TPU v7x, 128 devices: a whole 4x4x4 slice. The times are simulated.
128 devices in a mesh: section: 4 (over z), dp: 4 (over x_hi, core), tensor: 8 (over x_lo, y).
Axes of the slice: x: 4 (x_hi: 2, x_lo: 2; x = x_hi * 2 + x_lo), y: 4, z: 4, core: 2. Of those that a mesh axis runs over, the one named last changes fastest.
Arguments:
- inputs: bfloat16 [8, 128, 8192], P(None, 'dp', ('section', 'tensor')), may hold values from -6 to 6
- gate_wide: bfloat16 [8192, 14336], P('section', 'tensor'), may hold values from -0.0625 to 0.0625
- up_wide: bfloat16 [8192, 14336], P('section', 'tensor'), may hold values from -0.0625 to 0.0625
- down_wide: bfloat16 [14336, 8192], P('tensor', 'section'), may hold values from -0.09375 to 0.09375
- width_wide: int32 [1], replicated, may hold values from 7168 to 14336
- gate_narrow: bfloat16 [8192, 7168], P(('section', 'tensor'), 'dp'), may hold values from -0.0625 to 0.0625
- up_narrow: bfloat16 [8192, 7168], P(('section', 'tensor'), 'dp'), may hold values from -0.0625 to 0.0625
- down_narrow: bfloat16 [7168, 8192], P('dp', ('section', 'tensor')), may hold values from -0.125 to 0.125
- width_narrow: int32 [1], replicated, may hold values from 3584 to 7168
- cotangent: bfloat16 [8, 128, 8192], P('tensor', 'dp', 'section'), may hold values from -6 to 6
Outputs:
- outputs: bfloat16 [8, 128, 8192], P('tensor', 'dp', 'section')
- input_grad: bfloat16 [8, 128, 8192], P(None, 'dp', ('section', 'tensor'))
All inputs are finite; a program needn't handle non-finite values.
Results may differ from a plain program's by a relative error of at most 0.017.
Values may be sent and summed in bfloat16 or wider, within the bound.
No kernel may reach another device: no remote copies, remote signals or barrier semaphores. Data moves between devices by JAX's collectives and lax.ppermute only.
A program may use at most 128 MiB of HBM per device.

v0:
```python
import jax
import jax.numpy as jnp
from jax import lax
from jax.experimental import pallas as pl
from jax.experimental.pallas import tpu as pltpu
from jax.sharding import PartitionSpec as P

BF = jnp.bfloat16
F32 = jnp.float32
VMEM = 8 << 20
NT = (((1,), (1,)), ((), ()))


def ring(n, shift):
    return [(i, (i + shift) % n) for i in range(n)]


def send(parts, axis, n):
    return [lax.ppermute(p, axis, ring(n, r)) for r, p in zip(range(1, n), parts)]


def spread(own, axis, n):
    return [own] + send([own] * (n - 1), axis, n)


VM = pl.BlockSpec(memory_space=pltpu.VMEM)
SM = pl.BlockSpec(memory_space=pltpu.SMEM)


def fill_features(scratch, refs, t, mix, slot):
    width = refs[0].shape[1]
    for k, ref in enumerate(refs):
        owner = lax.rem(t - k + 8, 8)
        at = pl.multiple_of(slot(owner, mix) * width, width)
        scratch[:, pl.ds(at, width)] = ref[...]


def fill_rows(scratch, refs, me, n):
    rows = refs[0].shape[-2]
    for k, ref in enumerate(refs):
        at = pl.multiple_of(lax.rem(me - k + n, n) * rows, rows)
        if len(ref.shape) == 3:
            for g in range(2):
                scratch[g, pl.ds(at, rows), :] = ref[g]
        else:
            scratch[pl.ds(at, rows), :] = ref[...]


def plain_slot(owner, mix):
    return owner


def narrow_slot(owner, mix):
    return (((owner & 1) << 2) | (owner >> 1)) ^ mix


def narrow_owner(slot, mix):
    swapped = slot ^ mix
    return ((swapped & 3) << 1) | (swapped >> 2)


def call(kernel, idx, operands, outs, scratch, flops, moved):
    return pl.pallas_call(
        kernel,
        in_specs=[SM] + [VM] * len(operands),
        out_specs=[VM] * len(outs),
        out_shape=[pltpu.VMEM(shape, kind) for shape, kind in outs],
        scratch_shapes=scratch,
        compiler_params=pltpu.CompilerParams(vmem_limit_bytes=VMEM),
        cost_estimate=pl.CostEstimate(flops=flops, bytes_accessed=moved, transcendentals=0),
    )(idx, *operands)


def into_vmem(*weights):
    n = len(weights)

    def kernel(*refs):
        copies = [
            pltpu.make_async_copy(refs[i], refs[n + i], refs[2 * n].at[i]) for i in range(n)
        ]
        for c in copies:
            c.start()
        for c in copies:
            c.wait()

    moved = sum(w.size * 2 for w in weights)
    return pl.pallas_call(
        kernel,
        in_specs=[pl.BlockSpec(memory_space=pltpu.HBM)] * n,
        out_specs=[VM] * n,
        out_shape=[pltpu.VMEM(w.shape, w.dtype) for w in weights],
        scratch_shapes=[pltpu.SemaphoreType.DMA((n,))],
        compiler_params=pltpu.CompilerParams(vmem_limit_bytes=1 << 20),
        cost_estimate=pl.CostEstimate(flops=0, bytes_accessed=2 * moved, transcendentals=0),
    )(*weights)


def gate_up(idx, chunks, weights, narrow):
    tokens, width = chunks[0].shape
    feats = 8 * width
    units = weights[0].shape[-1]
    block = 256
    rows = tokens // 4
    mid_rows = tokens // 8
    n_w = len(weights)

    def kernel(idx_ref, *refs):
        xs, ws = refs[:8], refs[8 : 8 + n_w]
        outs = refs[8 + n_w : 12 + n_w]
        mid, lhs, val = refs[12 + n_w :]
        s, t, mix = idx_ref[0], idx_ref[1], idx_ref[2]
        fill_features(lhs, xs, t, mix, narrow_slot if narrow else plain_slot)
        if narrow:
            row = pl.multiple_of(t * mid_rows, mid_rows)
            for k, ref in enumerate(xs):
                owner = lax.rem(t - k + 8, 8)
                to = pl.multiple_of(owner * width, width)
                mid[:, pl.ds(to, width)] = ref[pl.ds(row, mid_rows), :]
        for g in range(2):
            for at in range(0, units, block):
                size = min(block, units - at)
                if narrow:
                    value = None
                    for j, w in enumerate(ws):
                        term = jnp.dot(
                            lhs[:, j * width : (j + 1) * width],
                            w[g, :, at : at + size],
                            preferred_element_type=F32,
                        )
                        value = term if value is None else value + term
                else:
                    value = jnp.dot(lhs[...], ws[g][:, at : at + size], preferred_element_type=F32)
                val[:, :size] = value
                for r, out in enumerate(outs):
                    row = pl.multiple_of(lax.rem(s + r, 4) * rows, rows)
                    out[g, :, at : at + size] = val[pl.ds(row, rows), :size].astype(out.dtype)

    res = call(
        kernel,
        idx,
        (*chunks, *weights),
        [((2, rows, units), F32)] + [((2, rows, units), BF)] * 3 + [((mid_rows, feats), BF)],
        [pltpu.VMEM((tokens, feats), BF), pltpu.VMEM((tokens, block), F32)],
        4 * tokens * feats * units,
        4 * feats * units,
    )
    return res[0], res[1:4], res[4]


def down_wide_part(idx, chunks, down_w):
    rows, units = chunks[0].shape
    tokens = 4 * rows
    feats = down_w.shape[1]
    width = feats // 8

    def kernel(idx_ref, *refs):
        hs, w, out, lhs = refs[:4], refs[4], refs[5], refs[6]
        fill_rows(lhs, hs, idx_ref[0], 4)
        for k in range(8):
            out[k] = jnp.dot(
                lhs[...], w[:, k * width : (k + 1) * width], preferred_element_type=F32
            ).astype(BF)

    return call(
        kernel,
        idx,
        (*chunks, down_w),
        [((8, tokens, width), BF)],
        [pltpu.VMEM((tokens, units), BF)],
        2 * tokens * feats * units,
        2 * feats * units,
    )[0]


def down_narrow_part(idx, chunks, weights):
    _, rows, units = chunks[0].shape
    tokens = 4 * rows
    width = weights[0].shape[1]
    feats = 8 * width

    def kernel(idx_ref, *refs):
        hs, ws, out, lhs = refs[:4], refs[4:12], refs[12], refs[13]
        mix = idx_ref[2]
        for k, h in enumerate(hs):
            row = pl.multiple_of(lax.rem(idx_ref[0] - k + 4, 4) * rows, rows)
            lhs[pl.ds(row, rows), :] = h[2]
        for j, w in enumerate(ws):
            at = pl.multiple_of(narrow_owner(j, mix) * width, width)
            out[:, pl.ds(at, width)] = lax.dot_general(
                lhs[...], w[2], NT, preferred_element_type=F32
            ).astype(BF)

    return call(
        kernel,
        idx,
        (*chunks, *weights),
        [((tokens, feats), BF)],
        [pltpu.VMEM((tokens, units), BF)],
        2 * tokens * feats * units,
        2 * feats * units,
    )[0]


def hidden_grad_wide(idx, chunks, down_w):
    tokens, width = chunks[0].shape
    feats = 8 * width
    units = down_w.shape[0]
    block = 256
    rows = tokens // 4

    def kernel(idx_ref, *refs):
        xs, w, outs, lhs, val = refs[:8], refs[8], refs[9:13], refs[13], refs[14]
        s, t = idx_ref[0], idx_ref[1]
        fill_features(lhs, xs, t, 0, plain_slot)
        for at in range(0, units, block):
            val[...] = lax.dot_general(
                lhs[...], w[at : at + block, :], NT, preferred_element_type=F32
            )
            for r, out in enumerate(outs):
                row = pl.multiple_of(lax.rem(s + r, 4) * rows, rows)
                out[:, at : at + block] = val[pl.ds(row, rows), :].astype(out.dtype)

    res = call(
        kernel,
        idx,
        (*chunks, down_w),
        [((rows, units), F32)] + [((rows, units), BF)] * 3,
        [pltpu.VMEM((tokens, feats), BF), pltpu.VMEM((tokens, block), F32)],
        2 * tokens * feats * units,
        2 * feats * units,
    )
    return res[0], res[1:]


def hidden_grad_narrow(idx, cot, weights):
    tokens, feats = cot.shape
    width = feats // 8
    units = weights[0].shape[2]
    block = 256
    rows = tokens // 4

    def kernel(idx_ref, *refs):
        lhs, ws, outs = refs[0], refs[1:9], refs[9:13]
        own, val = refs[13:]
        s, t, mix = idx_ref[0], idx_ref[1], idx_ref[2]
        own[...] = lhs[:, pl.ds(pl.multiple_of(t * width, width), width)]
        for at in range(0, units, block):
            size = min(block, units - at)
            total = None
            for j, w in enumerate(ws):
                left = lhs[:, pl.ds(pl.multiple_of(narrow_owner(j, mix) * width, width), width)]
                term = jnp.dot(left, w[2, :, at : at + size], preferred_element_type=F32)
                total = term if total is None else total + term
            val[:, :size] = total
            for r, out in enumerate(outs):
                row = pl.multiple_of(lax.rem(s + r, 4) * rows, rows)
                out[:, at : at + size] = val[pl.ds(row, rows), :size].astype(out.dtype)

    res = call(
        kernel,
        idx,
        (cot, *weights),
        [((rows, units), F32)] + [((rows, units), BF)] * 3 + [((tokens, width), BF)],
        [pltpu.VMEM((tokens, block), F32)],
        2 * tokens * feats * units,
        2 * feats * units,
    )
    return res[0], res[1:4], res[4]


def input_back_wide(idx, chunks, gate_w, up_w):
    _, rows, units = chunks[0].shape
    tokens = 4 * rows
    width = gate_w.shape[0] // 8
    feats = 8 * width

    def kernel(idx_ref, *refs):
        ps, g, u, out, lhs = refs[:4], refs[4], refs[5], refs[6], refs[7]
        fill_rows(lhs, ps, idx_ref[0], 4)
        for k in range(8):
            rows_k = slice(k * width, (k + 1) * width)
            value = lax.dot_general(lhs[0], g[rows_k, :], NT, preferred_element_type=F32)
            value += lax.dot_general(lhs[1], u[rows_k, :], NT, preferred_element_type=F32)
            out[k] = value.astype(BF)

    return call(
        kernel,
        idx,
        (*chunks, gate_w, up_w),
        [((8, tokens, width), BF)],
        [pltpu.VMEM((2, tokens, units), BF)],
        4 * tokens * feats * units,
        4 * feats * units,
    )[0]


def input_back_narrow(idx, chunks, weights):
    _, rows, units = chunks[0].shape
    tokens = 4 * rows
    width = weights[0].shape[1]
    feats = 8 * width

    def kernel(idx_ref, *refs):
        ps, ws, out, lhs = refs[:4], refs[4:12], refs[12], refs[13]
        mix = idx_ref[2]
        fill_rows(lhs, ps, idx_ref[0], 4)
        for j, w in enumerate(ws):
            value = lax.dot_general(lhs[0], w[0], NT, preferred_element_type=F32)
            value += lax.dot_general(lhs[1], w[1], NT, preferred_element_type=F32)
            out[narrow_owner(j, mix)] = value.astype(BF)

    return call(
        kernel,
        idx,
        (*chunks, *weights),
        [((8, tokens, width), BF)],
        [pltpu.VMEM((2, tokens, units), BF)],
        4 * tokens * feats * units,
        4 * feats * units,
    )[0]


def add_up(own, received):
    total = own
    for r in received:
        total = total + r.astype(F32)
    return total


def add_over_tensor(base, parts):
    received = lax.all_to_all(parts, "tensor", split_axis=0, concat_axis=0, tiled=True)
    return (base.astype(F32) + jnp.sum(received.astype(F32), axis=0)).astype(BF)


def hidden_of(gate, upper, mask):
    sigma = jax.nn.sigmoid(gate)
    return (gate * sigma * upper * mask).astype(BF)


def grads_of(dhid, gate, upper, mask):
    sigma = jax.nn.sigmoid(gate)
    dgate = (dhid * upper * sigma * (1.0 + gate * (1.0 - sigma)) * mask).astype(BF)
    dup = (dhid * gate * sigma * mask).astype(BF)
    return [dgate, dup]


def after(value, *earlier):
    return lax.optimization_barrier((value, earlier))[0]


CORES = [(0, 1), (1, 0), (2, 3), (3, 2)]


def own_halves(idx, gate_w, up_w, down_w):
    width, units = gate_w.shape
    size = units // 2

    def kernel(idx_ref, g, u, d, *outs):
        bit = (idx_ref[1] >> 1) & 1
        for j, out in enumerate(outs):
            at = pl.multiple_of((bit ^ j) * size, size)
            out[0] = g[:, pl.ds(at, size)]
            out[1] = u[:, pl.ds(at, size)]
            out[2] = d[pl.ds(at, size), :].T

    return call(
        kernel,
        idx,
        (gate_w, up_w, down_w),
        [((3, width, size), BF)] * 2,
        [],
        0,
        12 * width * units,
    )


def hand_out(piece, flip_x, flip_half):
    perm = []
    for d in range(4):
        for t in range(8):
            g, a, b = t >> 2, (t >> 1) & 1, t & 1
            to_d = (g ^ flip_x) * 2 + b
            to_t = 4 * (d & 1) + 2 * (d >> 1) + (a ^ flip_half)
            perm.append((d * 8 + t, to_d * 8 + to_t))
    return lax.ppermute(piece, ("dp", "tensor"), perm)


def to_sibling(pieces):
    return [lax.ppermute(p, "dp", CORES) for p in pieces]


def body(
    inputs,
    gate_wide,
    up_wide,
    down_wide,
    width_wide,
    gate_narrow,
    up_narrow,
    down_narrow,
    width_narrow,
    cotangent,
):
    section = lax.axis_index("section").astype(jnp.int32)
    tensor = lax.axis_index("tensor").astype(jnp.int32)
    dp = lax.axis_index("dp").astype(jnp.int32)
    mix = (dp & 1) * 4 + (dp >> 1) * 2 + (tensor & 1)
    idx = jnp.stack([section, tensor, mix])
    units_a = gate_wide.shape[1]
    units_b = gate_narrow.shape[1] // 2
    mask_a = (
        tensor * units_a + jnp.arange(units_a, dtype=jnp.int32) < width_wide[0]
    ).astype(F32)
    from_dp = 2 * ((tensor >> 1) & 1) + (tensor >> 2)
    mask_b = (
        (2 * from_dp + (tensor & 1)) * units_b + jnp.arange(units_b, dtype=jnp.int32) < width_narrow[0]
    ).astype(F32)
    blocks, quarter, width = inputs.shape
    tokens = blocks * quarter
    own_in = inputs.reshape(tokens, width)

    half = own_halves(idx, gate_narrow, up_narrow, down_narrow)
    cot_rows = lax.all_gather(cotangent[0], "tensor", axis=0, tiled=True)
    x_chunks = spread(own_in, "tensor", 8)
    gate_1, up_1 = into_vmem(*after((gate_wide, up_wide), x_chunks[1], x_chunks[2]))
    x_chunks = after(x_chunks, half)
    ready = after(half, x_chunks)
    a00, a11 = hand_out(ready[0], 0, 0), hand_out(ready[1], 1, 1)
    ready = after(half, (a00, a11))
    a01, a10 = hand_out(ready[1], 0, 1), hand_out(ready[0], 1, 0)

    own, parts, _ = gate_up(idx, x_chunks, (gate_1, up_1), False)
    down_1, = into_vmem(after(down_wide, own))
    both_a = add_up(own, send(parts, "section", 4))
    hidden_a = after(hidden_of(both_a[0], both_a[1], mask_a), (a00, a11))
    hidden_chunks = after(spread(hidden_a, "section", 4), down_1)
    s00, s11 = to_sibling(after([a00, a11], hidden_chunks))
    parts = after(down_wide_part(idx, hidden_chunks, down_1), (a01, a10))
    middle = add_over_tensor(own_in, parts)
    middle = after(middle, cot_rows)
    s01, s10 = to_sibling(after([a01, a10], middle))
    pieces = [a00, a01, a10, a11, s00, s01, s10, s11]
    mid_chunks = spread(middle, "tensor", 8)
    own, parts, cot_own = hidden_grad_narrow(idx, cot_rows, pieces)
    dhid_b = add_up(own, send(parts, "section", 4))
    mid_chunks = after(mid_chunks, cot_own)
    own, parts, mid_rows = gate_up(idx, mid_chunks, pieces, True)
    both_b = add_up(own, send(parts, "section", 4))

    hidden_b = hidden_of(both_b[0], both_b[1], mask_b)
    three_b = jnp.stack(grads_of(dhid_b, both_b[0], both_b[1], mask_b) + [hidden_b])
    three_chunks = spread(three_b, "section", 4)
    parts = input_back_narrow(idx, three_chunks, pieces)
    out_part = down_narrow_part(idx, after(three_chunks, parts), pieces)
    middle_grad = after(add_over_tensor(cot_own, parts), out_part)
    grad_chunks = spread(middle_grad, "tensor", 8)
    down_2, = into_vmem(after(down_wide, middle_grad))
    grad_chunks = after(grad_chunks, down_2)
    own, parts = hidden_grad_wide(idx, grad_chunks, down_2)

    received = send(parts, "section", 4)
    out_sum = lax.psum_scatter(after(out_part, own), "tensor", scatter_dimension=0, tiled=True)
    outputs = (mid_rows.astype(F32) + out_sum.astype(F32)).astype(BF)

    gate_2, = into_vmem(after(gate_wide, own))
    dhid_a = add_up(own, after(received, gate_2))
    pair_a = jnp.stack(grads_of(dhid_a, both_a[0], both_a[1], mask_a))
    up_2, = into_vmem(after(up_wide, dhid_a))
    pair_chunks = after(spread(pair_a, "section", 4), up_2)
    input_grad = add_over_tensor(middle_grad, input_back_wide(idx, pair_chunks, gate_2, up_2))
    return (
        outputs.reshape(1, quarter, outputs.shape[1]),
        input_grad.reshape(blocks, quarter, width),
    )


def solution(mesh):
    in_specs = (
        P(None, "dp", ("section", "tensor")),
        P("section", "tensor"),
        P("section", "tensor"),
        P("tensor", "section"),
        P(),
        P(("section", "tensor"), "dp"),
        P(("section", "tensor"), "dp"),
        P("dp", ("section", "tensor")),
        P(),
        P("tensor", "dp", "section"),
    )
    out_specs = (P("tensor", "dp", "section"), P(None, "dp", ("section", "tensor")))
    return jax.shard_map(body, mesh=mesh, in_specs=in_specs, out_specs=out_specs, check_vma=False)
```

profile of v0, /device:TPU:0, one launch (start us, length us, event | category | flops | bytes accessed | tf_op | source)
XLA Modules:
  0.0 325.1 jit_solution(9693832483626636810)
XLA Ops:
  8.9 2.9 collective-permute-start.1
  11.8 2.3 collective-permute-start.2
  16.6 3.2 collective-permute-start.5
  23.4 2.4 shard_map.113
  29.4 5.7 %collective-permute-start.11 = (bf16[3,256,896]{2,1,0:T(8,128)(2,1)}, bf16[3,256,896]{2,1,0:T(8,128)(2,1)S(1)}, u32[]{:S(2)}, u32[]{:S(2)}) collective-permute-start(bf16[3,256,896]{2,1,0:T(8,128)(2,1)} %get-tuple-element.108), channel_id=1, source_target_pairs={{0,17},{1,25},{2,16},{3,24},{4,1},{5,9},{6,0},{7,8},{8,21},{9,29},... | collective-permute-start | bytes 4128776 | tf_op jit(solution)/shard_map/ppermute | solution.py:385
  35.1 3.1 copy-done.2
  38.2 3.1 copy-done.4
  42.3 6.3 %shard_map.115 = (f32[2,64,1792]{2,1,0:T(8,128)S(1)}, bf16[2,64,1792]{2,1,0:T(8,128)(2,1)}, bf16[2,64,1792]{2,1,0:T(8,128)(2,1)}, bf16[2,64,1792]{2,1,0:T(8,128)(2,1)}, bf16[32,2048]{1,0:T(8,128)(2,1)}) custom-call(s32[3]{0:T(128)S(1)} %pad_add_fusion.idx_ref, bf16[256,256]{1,0:T(8,128)(2,1)S(1)} %bitcast.91, ...), custom_call_target="tpu_custom_call" | custom-call | flops 3758096384 | bytes 14680064 | tf_op jit(solution)/shard_map/pallas_call | solution.py:63
  49.5 4.0 %collective-permute-start.9 = (bf16[2,64,1792]{2,1,0:T(8,128)(2,1)}, bf16[2,64,1792]{2,1,0:T(8,128)(2,1)S(1)}, u32[]{:S(2)}, u32[]{:S(2)}) collective-permute-start(bf16[2,64,1792]{2,1,0:T(8,128)(2,1)} %get-tuple-element.99), channel_id=1, source_target_pairs={{0,96},{32,0},{64,32},{96,64},{1,97},{33,1},{65,33},{97,65},{2,98}... | collective-permute-start | bytes 1376264 | tf_op jit(solution)/shard_map/ppermute | solution.py:19
  55.5 14.1 %collective-permute-done.11.refs_4_.refs_11_.refs_7_ = bf16[3,256,896]{2,1,0:T(8,128)(2,1)S(1)} collective-permute-done((bf16[3,256,896]{2,1,0:T(8,128)(2,1)}, bf16[3,256,896]{2,1,0:T(8,128)(2,1)S(1)}, u32[]{:S(2)}, u32[]{:S(2)}) %collective-permute-start.11) | collective-permute-done | bytes 1376288 | tf_op jit(solution)/shard_map/ppermute | solution.py:385
  70.2 5.5 %collective-permute-start.16 = (bf16[3,256,896]{2,1,0:T(8,128)(2,1)}, bf16[3,256,896]{2,1,0:T(8,128)(2,1)}, u32[]{:S(2)}, u32[]{:S(2)}) collective-permute-start(bf16[3,256,896]{2,1,0:T(8,128)(2,1)} %get-tuple-element.109), channel_id=1, source_target_pairs={{0,16},{1,24},{2,17},{3,25},{4,0},{5,8},{6,1},{7,9},{8,20},{9,28},... | collective-permute-start | bytes 4128776 | tf_op jit(solution)/shard_map/ppermute | solution.py:385
  79.7 3.7 %collective-permute-start.13 = (bf16[64,1792]{1,0:T(8,128)(2,1)S(1)}, bf16[64,1792]{1,0:T(8,128)(2,1)S(1)}, u32[]{:S(2)}, u32[]{:S(2)}) collective-permute-start(bf16[64,1792]{1,0:T(8,128)(2,1)S(1)} %multiply_convert_fusion.2.refs_0_), channel_id=1, source_target_pairs={{0,64},{32,96},{64,0},{96,32},{1,65},{33,97},{65,1},{97,33},{2,66}... | collective-permute-start | bytes 688136 | tf_op jit(solution)/shard_map/ppermute | solution.py:19
  84.4 3.1 copy-done
  89.3 2.5 collective-permute-done.13.refs_2_
  92.3 2.7 shard_map.117
  95.0 12.6 %collective-permute-done.15.refs_2_.refs_9_.refs_5_ = bf16[3,256,896]{2,1,0:T(8,128)(2,1)} collective-permute-done((bf16[3,256,896]{2,1,0:T(8,128)(2,1)}, bf16[3,256,896]{2,1,0:T(8,128)(2,1)}, u32[]{:S(2)}, u32[]{:S(2)}) %collective-permute-start.15) | collective-permute-done | bytes 1376288 | tf_op jit(solution)/shard_map/ppermute | solution.py:385
  107.6 13.1 %all-to-all-start = ((bf16[8,256,256]{2,1,0:T(8,128)(2,1)}), bf16[8,256,256]{2,1,0:T(8,128)(2,1)}, u32[]{:S(2)}, u32[]{:S(2)}) async-start(bf16[8,256,256]{2,1,0:T(8,128)(2,1)} %copy-done.13), calls=%async_computation | async-start | bytes 2097152 | tf_op jit(solution)/shard_map/all_to_all | solution.py:331
  121.2 10.2 %all-to-all-done = bf16[8,256,256]{2,1,0:T(8,128)(2,1)} async-done(((bf16[8,256,256]{2,1,0:T(8,128)(2,1)}), bf16[8,256,256]{2,1,0:T(8,128)(2,1)}, u32[]{:S(2)}, u32[]{:S(2)}) %all-to-all-start) | async-done | bytes 1048608 | tf_op jit(solution)/shard_map/all_to_all | solution.py:331
  134.3 2.5 collective-permute-start.18
  137.9 5.3 %collective-permute-done.17.refs_1_ = bf16[256,256]{1,0:T(8,128)(2,1)S(1)} collective-permute-done((bf16[256,256]{1,0:T(8,128)(2,1)S(1)}, bf16[256,256]{1,0:T(8,128)(2,1)S(1)}, u32[]{:S(2)}, u32[]{:S(2)}) %collective-permute-start.17) | collective-permute-done | bytes 131104 | tf_op jit(solution)/shard_map/ppermute | solution.py:19
  144.6 2.7 collective-permute-start.21
  147.3 2.2 collective-permute-start.22
  151.3 4.0 %shard_map.118 = (f32[64,896]{1,0:T(8,128)S(1)}, bf16[64,896]{1,0:T(8,128)(2,1)S(1)}, bf16[64,896]{1,0:T(8,128)(2,1)S(1)}, bf16[64,896]{1,0:T(8,128)(2,1)S(1)}, bf16[256,256]{1,0:T(8,128)(2,1)S(1)}) custom-call(s32[3]{0:T(128)S(1)} %pad_add_fusion.idx_ref, bf16[256,2048]{1,0:T(8,128)(2,1)S(1)} %bitcast.83, ...), custom_call_target="tpu_custom_call" | custom-call | flops 939524096 | bytes 3670016 | tf_op jit(solution)/shard_map/pallas_call | solution.py:63
  155.4 6.3 %shard_map.119 = (f32[2,64,896]{2,1,0:T(8,128)S(1)}, bf16[2,64,896]{2,1,0:T(8,128)(2,1)}, bf16[2,64,896]{2,1,0:T(8,128)(2,1)}, bf16[2,64,896]{2,1,0:T(8,128)(2,1)}, bf16[32,2048]{1,0:T(8,128)(2,1)S(1)}) custom-call(s32[3]{0:T(128)S(1)} %pad_add_fusion.idx_ref, bf16[256,256]{1,0:T(8,128)(2,1)S(1)} %add_convert_fusion.3.refs_0_, ...), custom_call_target="tpu_custom_call" | custom-call | flops 1879048192 | bytes 7340032 | tf_op jit(solution)/shard_map/pallas_call | solution.py:63
  162.4 4.5 %collective-permute-start.33 = (bf16[2,64,896]{2,1,0:T(8,128)(2,1)}, bf16[2,64,896]{2,1,0:T(8,128)(2,1)}, u32[]{:S(2)}, u32[]{:S(2)}) collective-permute-start(bf16[2,64,896]{2,1,0:T(8,128)(2,1)} %get-tuple-element.133), channel_id=1, source_target_pairs={{0,96},{32,0},{64,32},{96,64},{1,97},{33,1},{65,33},{97,65},{2,98}... | collective-permute-start | bytes 688136 | tf_op jit(solution)/shard_map/ppermute | solution.py:19
  173.3 6.0 %collective-permute-done.33 = bf16[2,64,896]{2,1,0:T(8,128)(2,1)} collective-permute-done((bf16[2,64,896]{2,1,0:T(8,128)(2,1)}, bf16[2,64,896]{2,1,0:T(8,128)(2,1)}, u32[]{:S(2)}, u32[]{:S(2)}) %collective-permute-start.33) | collective-permute-done | bytes 229408 | tf_op jit(solution)/shard_map/ppermute | solution.py:19
  182.9 3.4 %collective-permute-done.28 = bf16[64,896]{1,0:T(8,128)(2,1)S(1)} collective-permute-done((bf16[64,896]{1,0:T(8,128)(2,1)}, bf16[64,896]{1,0:T(8,128)(2,1)S(1)}, u32[]{:S(2)}, u32[]{:S(2)}) %collective-permute-start.28) | collective-permute-done | bytes 114720 | tf_op jit(solution)/shard_map/ppermute | solution.py:19
  186.7 4.2 %collective-permute-start.35 = (bf16[3,64,896]{2,1,0:T(8,128)(2,1)S(1)}, bf16[3,64,896]{2,1,0:T(8,128)(2,1)S(1)}, u32[]{:S(2)}, u32[]{:S(2)}) collective-permute-start(bf16[3,64,896]{2,1,0:T(8,128)(2,1)S(1)} %pad_maximum_fusion.1.refs_0_), channel_id=1, source_target_pairs={{0,64},{32,96},{64,0},{96,32},{1,65},{33,97},{65,1},{97,33},{2,66}... | collective-permute-start | bytes 1032200 | tf_op jit(solution)/shard_map/ppermute | solution.py:19
  191.2 6.7 %collective-permute-done.34.refs_1_ = bf16[3,64,896]{2,1,0:T(8,128)(2,1)S(1)} collective-permute-done((bf16[3,64,896]{2,1,0:T(8,128)(2,1)S(1)}, bf16[3,64,896]{2,1,0:T(8,128)(2,1)S(1)}, u32[]{:S(2)}, u32[]{:S(2)}) %collective-permute-start.34) | collective-permute-done | bytes 344096 | tf_op jit(solution)/shard_map/ppermute | solution.py:19
  197.9 3.7 %collective-permute-done.35.refs_2_ = bf16[3,64,896]{2,1,0:T(8,128)(2,1)S(1)} collective-permute-done((bf16[3,64,896]{2,1,0:T(8,128)(2,1)S(1)}, bf16[3,64,896]{2,1,0:T(8,128)(2,1)S(1)}, u32[]{:S(2)}, u32[]{:S(2)}) %collective-permute-start.35) | collective-permute-done | bytes 344096 | tf_op jit(solution)/shard_map/ppermute | solution.py:19
  201.6 5.0 %shard_map.120 = bf16[8,256,256]{2,1,0:T(8,128)(2,1)S(1)} custom-call(s32[3]{0:T(128)S(1)} %pad_add_fusion.idx_ref, bf16[3,64,896]{2,1,0:T(8,128)(2,1)S(1)} %pad_maximum_fusion.1.refs_0_, bf16[3,64,896]{2,1,0:T(8,128)(2,1)S(1)} %collective-permute-done.34.refs_1_, bf16[3,64,896]{2,1,0:T(8,128)(2,1)S(1)} %collective-permute-done.35.refs_2_, ...), custom_call_target="tpu_custom_call" | custom-call | flops 1879048192 | bytes 7340032 | tf_op jit(solution)/shard_map/pallas_call | solution.py:63
  209.1 5.5 %all-to-all-start.1 = ((bf16[8,256,256]{2,1,0:T(8,128)(2,1)}), bf16[8,256,256]{2,1,0:T(8,128)(2,1)}, u32[]{:S(2)}, u32[]{:S(2)}) async-start(bf16[8,256,256]{2,1,0:T(8,128)(2,1)} %copy-done.15), calls=%async_computation.1 | async-start | bytes 2097152 | tf_op jit(solution)/shard_map/all_to_all | solution.py:331
  219.2 3.9 %shard_map.121 = bf16[256,2048]{1,0:T(8,128)(2,1)S(1)} custom-call(s32[3]{0:T(128)S(1)} %pad_add_fusion.idx_ref, bf16[3,64,896]{2,1,0:T(8,128)(2,1)S(1)} %pad_maximum_fusion.1.refs_0_, bf16[3,64,896]{2,1,0:T(8,128)(2,1)S(1)} %collective-permute-done.34.refs_1_, bf16[3,64,896]{2,1,0:T(8,128)(2,1)S(1)} %copy-done.17, bf16[3,64,896]{2,1,0:T(8,128)(2,1)S(1)} %copy-done.19, ...), custom_call_target="tpu_custom_call" | custom-call | flops 939524096 | bytes 3670016 | tf_op jit(solution)/shard_map/pallas_call | solution.py:63
  224.1 3.0 all-to-all-done.1
  230.4 2.4 collective-permute-start.38
  239.0 2.4 collective-permute-start.43
  241.4 3.1 copy-done.1
  245.0 2.0 collective-permute-done.42.refs_6_
  247.1 2.9 shard_map.123
  250.0 2.4 collective-permute-start.44
  252.5 2.7 collective-permute-start.45
  255.5 3.1 copy-done.3
  259.1 3.0 copy-done.6
  267.8 3.1 copy-done.5
  271.4 7.0 %collective-permute-done.47.refs_1_ = bf16[2,64,1792]{2,1,0:T(8,128)(2,1)} collective-permute-done((bf16[2,64,1792]{2,1,0:T(8,128)(2,1)}, bf16[2,64,1792]{2,1,0:T(8,128)(2,1)}, u32[]{:S(2)}, u32[]{:S(2)}) %collective-permute-start.47) | collective-permute-done | bytes 458784 | tf_op jit(solution)/shard_map/ppermute | solution.py:19
  278.3 4.9 %collective-permute-done.48.refs_2_ = bf16[2,64,1792]{2,1,0:T(8,128)(2,1)} collective-permute-done((bf16[2,64,1792]{2,1,0:T(8,128)(2,1)}, bf16[2,64,1792]{2,1,0:T(8,128)(2,1)}, u32[]{:S(2)}, u32[]{:S(2)}) %collective-permute-start.48) | collective-permute-done | bytes 458784 | tf_op jit(solution)/shard_map/ppermute | solution.py:19
  283.5 5.4 %shard_map.126 = bf16[8,256,256]{2,1,0:T(8,128)(2,1)S(1)} custom-call(s32[3]{0:T(128)S(1)} %pad_add_fusion.idx_ref, bf16[2,64,1792]{2,1,0:T(8,128)(2,1)} %pad_maximum_fusion.refs_0_, bf16[2,64,1792]{2,1,0:T(8,128)(2,1)} %collective-permute-done.47.refs_1_, bf16[2,64,1792]{2,1,0:T(8,128)(2,1)} %collective-permute-done.48.refs_2_, ...), custom_call_target="tpu_custom_call" | custom-call | flops 3758096384 | bytes 14680064 | tf_op jit(solution)/shard_map/pallas_call | solution.py:63
  288.9 26.9 %all_to_all.15 = bf16[8,256,256]{2,1,0:T(8,128)(2,1)S(1)} all-to-all(bf16[8,256,256]{2,1,0:T(8,128)(2,1)S(1)} %shard_map.126), channel_id=1, replica_groups=mesh['section'=4,'dp'=4,'tensor'=8] {'tensor'}, dimensions={0} | all-to-all | bytes 2097152 | tf_op jit(solution)/shard_map/all_to_all | solution.py:331
  (181 shorter events, 68.5 us)
Async XLA Ops:
  7.2 125.7 %all-gather.3.cloned.1.call-start = ((), (), s32[]{:S(2)}) async-start(), calls=%async_computation.5 | async-start | bytes 1179648 | tf_op jit(solution)/shard_map/all_gather | solution.py:423
  7.2 9.4 %collective-permute-start = (bf16[256,256]{1,0:T(8,128)(2,1)}, bf16[256,256]{1,0:T(8,128)(2,1)S(1)}, u32[]{:S(2)}, u32[]{:S(2)}) collective-permute-start(bf16[256,256]{1,0:T(8,128)(2,1)} %bitcast.84), channel_id=1, source_target_pairs={{0,1},{1,2},{2,3},{3,4},{4,5},{5,6},{6,7},{7,0},{8,9},{9,10},{10,1... | collective-permute-start | bytes 393224 | tf_op jit(solution)/shard_map/ppermute | solution.py:19
  8.9 10.8 %collective-permute-start.1 = (bf16[256,256]{1,0:T(8,128)(2,1)}, bf16[256,256]{1,0:T(8,128)(2,1)S(1)}, u32[]{:S(2)}, u32[]{:S(2)}) collective-permute-start(bf16[256,256]{1,0:T(8,128)(2,1)} %bitcast.85), channel_id=1, source_target_pairs={{0,2},{1,3},{2,4},{3,5},{4,6},{5,7},{6,0},{7,1},{8,10},{9,11},{10,... | collective-permute-start | bytes 393224 | tf_op jit(solution)/shard_map/ppermute | solution.py:19
  11.8 13.9 %collective-permute-start.2 = (bf16[256,256]{1,0:T(8,128)(2,1)}, bf16[256,256]{1,0:T(8,128)(2,1)S(1)}, u32[]{:S(2)}, u32[]{:S(2)}) collective-permute-start(bf16[256,256]{1,0:T(8,128)(2,1)} %bitcast.86), channel_id=1, source_target_pairs={{0,3},{1,4},{2,5},{3,6},{4,7},{5,0},{6,1},{7,2},{8,11},{9,12},{10,... | collective-permute-start | bytes 393224 | tf_op jit(solution)/shard_map/ppermute | solution.py:19
  14.1 11.6 %collective-permute-start.3 = (bf16[256,256]{1,0:T(8,128)(2,1)}, bf16[256,256]{1,0:T(8,128)(2,1)S(1)}, u32[]{:S(2)}, u32[]{:S(2)}) collective-permute-start(bf16[256,256]{1,0:T(8,128)(2,1)} %bitcast.87), channel_id=1, source_target_pairs={{0,4},{1,5},{2,6},{3,7},{4,0},{5,1},{6,2},{7,3},{8,12},{9,13},{10,... | collective-permute-start | bytes 393224 | tf_op jit(solution)/shard_map/ppermute | solution.py:19
  14.7 11.1 %collective-permute-start.4 = (bf16[256,256]{1,0:T(8,128)(2,1)}, bf16[256,256]{1,0:T(8,128)(2,1)S(1)}, u32[]{:S(2)}, u32[]{:S(2)}) collective-permute-start(bf16[256,256]{1,0:T(8,128)(2,1)} %bitcast.88), channel_id=1, source_target_pairs={{0,5},{1,6},{2,7},{3,0},{4,1},{5,2},{6,3},{7,4},{8,13},{9,14},{10,... | collective-permute-start | bytes 393224 | tf_op jit(solution)/shard_map/ppermute | solution.py:19
  16.6 9.2 %collective-permute-start.5 = (bf16[256,256]{1,0:T(8,128)(2,1)}, bf16[256,256]{1,0:T(8,128)(2,1)S(1)}, u32[]{:S(2)}, u32[]{:S(2)}) collective-permute-start(bf16[256,256]{1,0:T(8,128)(2,1)} %bitcast.89), channel_id=1, source_target_pairs={{0,6},{1,7},{2,0},{3,1},{4,2},{5,3},{6,4},{7,5},{8,14},{9,15},{10,... | collective-permute-start | bytes 393224 | tf_op jit(solution)/shard_map/ppermute | solution.py:19
  27.4 28.1 %collective-permute-start.10 = (bf16[3,256,896]{2,1,0:T(8,128)(2,1)}, bf16[3,256,896]{2,1,0:T(8,128)(2,1)S(1)}, u32[]{:S(2)}, u32[]{:S(2)}) collective-permute-start(bf16[3,256,896]{2,1,0:T(8,128)(2,1)} %get-tuple-element.109), channel_id=1, source_target_pairs={{0,0},{1,8},{2,1},{3,9},{4,16},{5,24},{6,17},{7,25},{8,4},{9,12},{... | collective-permute-start | bytes 4128776 | tf_op jit(solution)/shard_map/ppermute | solution.py:385
  29.4 40.2 %collective-permute-start.11 = (bf16[3,256,896]{2,1,0:T(8,128)(2,1)}, bf16[3,256,896]{2,1,0:T(8,128)(2,1)S(1)}, u32[]{:S(2)}, u32[]{:S(2)}) collective-permute-start(bf16[3,256,896]{2,1,0:T(8,128)(2,1)} %get-tuple-element.108), channel_id=1, source_target_pairs={{0,17},{1,25},{2,16},{3,24},{4,1},{5,9},{6,0},{7,8},{8,21},{9,29},... | collective-permute-start | bytes 4128776 | tf_op jit(solution)/shard_map/ppermute | solution.py:385
  49.5 26.1 %collective-permute-start.9 = (bf16[2,64,1792]{2,1,0:T(8,128)(2,1)}, bf16[2,64,1792]{2,1,0:T(8,128)(2,1)S(1)}, u32[]{:S(2)}, u32[]{:S(2)}) collective-permute-start(bf16[2,64,1792]{2,1,0:T(8,128)(2,1)} %get-tuple-element.99), channel_id=1, source_target_pairs={{0,96},{32,0},{64,32},{96,64},{1,97},{33,1},{65,33},{97,65},{2,98}... | collective-permute-start | bytes 1376264 | tf_op jit(solution)/shard_map/ppermute | solution.py:19
  53.6 22.1 %collective-permute-start.8 = (bf16[2,64,1792]{2,1,0:T(8,128)(2,1)}, bf16[2,64,1792]{2,1,0:T(8,128)(2,1)}, u32[]{:S(2)}, u32[]{:S(2)}) collective-permute-start(bf16[2,64,1792]{2,1,0:T(8,128)(2,1)} %get-tuple-element.98), channel_id=1, source_target_pairs={{0,64},{32,96},{64,0},{96,32},{1,65},{33,97},{65,1},{97,33},{2,66}... | collective-permute-start | bytes 1376264 | tf_op jit(solution)/shard_map/ppermute | solution.py:19
  53.6 23.0 %collective-permute-start.7 = (bf16[2,64,1792]{2,1,0:T(8,128)(2,1)}, bf16[2,64,1792]{2,1,0:T(8,128)(2,1)}, u32[]{:S(2)}, u32[]{:S(2)}) collective-permute-start(bf16[2,64,1792]{2,1,0:T(8,128)(2,1)} %get-tuple-element.97), channel_id=1, source_target_pairs={{0,32},{32,64},{64,96},{96,0},{1,33},{33,65},{65,97},{97,1},{2,34}... | collective-permute-start | bytes 1376264 | tf_op jit(solution)/shard_map/ppermute | solution.py:19
  69.6 38.0 %collective-permute-start.15 = (bf16[3,256,896]{2,1,0:T(8,128)(2,1)}, bf16[3,256,896]{2,1,0:T(8,128)(2,1)}, u32[]{:S(2)}, u32[]{:S(2)}) collective-permute-start(bf16[3,256,896]{2,1,0:T(8,128)(2,1)} %get-tuple-element.108), channel_id=1, source_target_pairs={{0,1},{1,9},{2,0},{3,8},{4,17},{5,25},{6,16},{7,24},{8,5},{9,13},{... | collective-permute-start | bytes 4128776 | tf_op jit(solution)/shard_map/ppermute | solution.py:385
  70.2 37.5 %collective-permute-start.16 = (bf16[3,256,896]{2,1,0:T(8,128)(2,1)}, bf16[3,256,896]{2,1,0:T(8,128)(2,1)}, u32[]{:S(2)}, u32[]{:S(2)}) collective-permute-start(bf16[3,256,896]{2,1,0:T(8,128)(2,1)} %get-tuple-element.109), channel_id=1, source_target_pairs={{0,16},{1,24},{2,17},{3,25},{4,0},{5,8},{6,1},{7,9},{8,20},{9,28},... | collective-permute-start | bytes 4128776 | tf_op jit(solution)/shard_map/ppermute | solution.py:385
  78.4 10.9 %collective-permute-start.12 = (bf16[64,1792]{1,0:T(8,128)(2,1)S(1)}, bf16[64,1792]{1,0:T(8,128)(2,1)S(1)}, u32[]{:S(2)}, u32[]{:S(2)}) collective-permute-start(bf16[64,1792]{1,0:T(8,128)(2,1)S(1)} %multiply_convert_fusion.2.refs_0_), channel_id=1, source_target_pairs={{0,32},{32,64},{64,96},{96,0},{1,33},{33,65},{65,97},{97,1},{2,34}... | collective-permute-start | bytes 688136 | tf_op jit(solution)/shard_map/ppermute | solution.py:19
  79.7 12.1 %collective-permute-start.13 = (bf16[64,1792]{1,0:T(8,128)(2,1)S(1)}, bf16[64,1792]{1,0:T(8,128)(2,1)S(1)}, u32[]{:S(2)}, u32[]{:S(2)}) collective-permute-start(bf16[64,1792]{1,0:T(8,128)(2,1)S(1)} %multiply_convert_fusion.2.refs_0_), channel_id=1, source_target_pairs={{0,64},{32,96},{64,0},{96,32},{1,65},{33,97},{65,1},{97,33},{2,66}... | collective-permute-start | bytes 688136 | tf_op jit(solution)/shard_map/ppermute | solution.py:19
  83.4 9.0 %collective-permute-start.14 = (bf16[64,1792]{1,0:T(8,128)(2,1)S(1)}, bf16[64,1792]{1,0:T(8,128)(2,1)S(1)}, u32[]{:S(2)}, u32[]{:S(2)}) collective-permute-start(bf16[64,1792]{1,0:T(8,128)(2,1)S(1)} %multiply_convert_fusion.2.refs_0_), channel_id=1, source_target_pairs={{0,96},{32,0},{64,32},{96,64},{1,97},{33,1},{65,33},{97,65},{2,98}... | collective-permute-start | bytes 688136 | tf_op jit(solution)/shard_map/ppermute | solution.py:19
  107.6 23.8 %all-to-all-start = ((bf16[8,256,256]{2,1,0:T(8,128)(2,1)}), bf16[8,256,256]{2,1,0:T(8,128)(2,1)}, u32[]{:S(2)}, u32[]{:S(2)}) async-start(bf16[8,256,256]{2,1,0:T(8,128)(2,1)} %copy-done.13), calls=%async_computation | async-start | bytes 2097152 | tf_op jit(solution)/shard_map/all_to_all | solution.py:331
  120.7 13.6 %collective-permute-start.24 = (bf16[3,256,896]{2,1,0:T(8,128)(2,1)S(1)}, bf16[3,256,896]{2,1,0:T(8,128)(2,1)}, u32[]{:S(2)}, u32[]{:S(2)}) collective-permute-start(bf16[3,256,896]{2,1,0:T(8,128)(2,1)S(1)} %collective-permute-done.10.refs_1_.refs_8_.refs_4_), channel_id=1, source_target_pairs={{0,8},{8,0},{16,24},{24,16},{1,9},{9,1},{17,25},{25,17},{2,10},{10... | collective-permute-start | bytes 4128776 | tf_op jit(solution)/shard_map/ppermute | solution.py:389
  120.7 16.1 %collective-permute-start.27 = (bf16[3,256,896]{2,1,0:T(8,128)(2,1)S(1)}, bf16[3,256,896]{2,1,0:T(8,128)(2,1)}, u32[]{:S(2)}, u32[]{:S(2)}) collective-permute-start(bf16[3,256,896]{2,1,0:T(8,128)(2,1)S(1)} %collective-permute-done.11.refs_4_.refs_11_.refs_7_), channel_id=1, source_target_pairs={{0,8},{8,0},{16,24},{24,16},{1,9},{9,1},{17,25},{25,17},{2,10},{10... | collective-permute-start | bytes 4128776 | tf_op jit(solution)/shard_map/ppermute | solution.py:389
  132.9 14.5 %collective-permute-start.25 = (bf16[3,256,896]{2,1,0:T(8,128)(2,1)}, bf16[3,256,896]{2,1,0:T(8,128)(2,1)S(1)}, u32[]{:S(2)}, u32[]{:S(2)}) collective-permute-start(bf16[3,256,896]{2,1,0:T(8,128)(2,1)} %collective-permute-done.15.refs_2_.refs_9_.refs_5_), channel_id=1, source_target_pairs={{0,8},{8,0},{16,24},{24,16},{1,9},{9,1},{17,25},{25,17},{2,10},{10... | collective-permute-start | bytes 4128776 | tf_op jit(solution)/shard_map/ppermute | solution.py:389
  133.0 16.5 %collective-permute-start.26 = (bf16[3,256,896]{2,1,0:T(8,128)(2,1)}, bf16[3,256,896]{2,1,0:T(8,128)(2,1)S(1)}, u32[]{:S(2)}, u32[]{:S(2)}) collective-permute-start(bf16[3,256,896]{2,1,0:T(8,128)(2,1)} %collective-permute-done.16.refs_3_.refs_10_.refs_6_), channel_id=1, source_target_pairs={{0,8},{8,0},{16,24},{24,16},{1,9},{9,1},{17,25},{25,17},{2,10},{10... | collective-permute-start | bytes 4128776 | tf_op jit(solution)/shard_map/ppermute | solution.py:389
  133.5 9.7 %collective-permute-start.17 = (bf16[256,256]{1,0:T(8,128)(2,1)S(1)}, bf16[256,256]{1,0:T(8,128)(2,1)S(1)}, u32[]{:S(2)}, u32[]{:S(2)}) collective-permute-start(bf16[256,256]{1,0:T(8,128)(2,1)S(1)} %add_convert_fusion.3.refs_0_), channel_id=1, source_target_pairs={{0,1},{1,2},{2,3},{3,4},{4,5},{5,6},{6,7},{7,0},{8,9},{9,10},{10,1... | collective-permute-start | bytes 393224 | tf_op jit(solution)/shard_map/ppermute | solution.py:19
  134.3 10.3 %collective-permute-start.18 = (bf16[256,256]{1,0:T(8,128)(2,1)S(1)}, bf16[256,256]{1,0:T(8,128)(2,1)S(1)}, u32[]{:S(2)}, u32[]{:S(2)}) collective-permute-start(bf16[256,256]{1,0:T(8,128)(2,1)S(1)} %add_convert_fusion.3.refs_0_), channel_id=1, source_target_pairs={{0,2},{1,3},{2,4},{3,5},{4,6},{5,7},{6,0},{7,1},{8,10},{9,11},{10,... | collective-permute-start | bytes 393224 | tf_op jit(solution)/shard_map/ppermute | solution.py:19
  136.8 18.5 %collective-permute-start.19 = (bf16[256,256]{1,0:T(8,128)(2,1)S(1)}, bf16[256,256]{1,0:T(8,128)(2,1)S(1)}, u32[]{:S(2)}, u32[]{:S(2)}) collective-permute-start(bf16[256,256]{1,0:T(8,128)(2,1)S(1)} %add_convert_fusion.3.refs_0_), channel_id=1, source_target_pairs={{0,3},{1,4},{2,5},{3,6},{4,7},{5,0},{6,1},{7,2},{8,11},{9,12},{10,... | collective-permute-start | bytes 393224 | tf_op jit(solution)/shard_map/ppermute | solution.py:19
  143.2 12.2 %collective-permute-start.20 = (bf16[256,256]{1,0:T(8,128)(2,1)S(1)}, bf16[256,256]{1,0:T(8,128)(2,1)S(1)}, u32[]{:S(2)}, u32[]{:S(2)}) collective-permute-start(bf16[256,256]{1,0:T(8,128)(2,1)S(1)} %add_convert_fusion.3.refs_0_), channel_id=1, source_target_pairs={{0,4},{1,5},{2,6},{3,7},{4,0},{5,1},{6,2},{7,3},{8,12},{9,13},{10,... | collective-permute-start | bytes 393224 | tf_op jit(solution)/shard_map/ppermute | solution.py:19
  144.6 10.8 %collective-permute-start.21 = (bf16[256,256]{1,0:T(8,128)(2,1)S(1)}, bf16[256,256]{1,0:T(8,128)(2,1)S(1)}, u32[]{:S(2)}, u32[]{:S(2)}) collective-permute-start(bf16[256,256]{1,0:T(8,128)(2,1)S(1)} %add_convert_fusion.3.refs_0_), channel_id=1, source_target_pairs={{0,5},{1,6},{2,7},{3,0},{4,1},{5,2},{6,3},{7,4},{8,13},{9,14},{10,... | collective-permute-start | bytes 393224 | tf_op jit(solution)/shard_map/ppermute | solution.py:19
  162.4 16.8 %collective-permute-start.33 = (bf16[2,64,896]{2,1,0:T(8,128)(2,1)}, bf16[2,64,896]{2,1,0:T(8,128)(2,1)}, u32[]{:S(2)}, u32[]{:S(2)}) collective-permute-start(bf16[2,64,896]{2,1,0:T(8,128)(2,1)} %get-tuple-element.133), channel_id=1, source_target_pairs={{0,96},{32,0},{64,32},{96,64},{1,97},{33,1},{65,33},{97,65},{2,98}... | collective-permute-start | bytes 688136 | tf_op jit(solution)/shard_map/ppermute | solution.py:19
  167.0 12.3 %collective-permute-start.32 = (bf16[2,64,896]{2,1,0:T(8,128)(2,1)}, bf16[2,64,896]{2,1,0:T(8,128)(2,1)}, u32[]{:S(2)}, u32[]{:S(2)}) collective-permute-start(bf16[2,64,896]{2,1,0:T(8,128)(2,1)} %get-tuple-element.132), channel_id=1, source_target_pairs={{0,64},{32,96},{64,0},{96,32},{1,65},{33,97},{65,1},{97,33},{2,66}... | collective-permute-start | bytes 688136 | tf_op jit(solution)/shard_map/ppermute | solution.py:19
  167.7 13.6 %collective-permute-start.31 = (bf16[2,64,896]{2,1,0:T(8,128)(2,1)}, bf16[2,64,896]{2,1,0:T(8,128)(2,1)}, u32[]{:S(2)}, u32[]{:S(2)}) collective-permute-start(bf16[2,64,896]{2,1,0:T(8,128)(2,1)} %get-tuple-element.131), channel_id=1, source_target_pairs={{0,32},{32,64},{64,96},{96,0},{1,33},{33,65},{65,97},{97,1},{2,34}... | collective-permute-start | bytes 688136 | tf_op jit(solution)/shard_map/ppermute | solution.py:19
  169.8 12.8 %collective-permute-start.30 = (bf16[64,896]{1,0:T(8,128)(2,1)}, bf16[64,896]{1,0:T(8,128)(2,1)S(1)}, u32[]{:S(2)}, u32[]{:S(2)}) collective-permute-start(bf16[64,896]{1,0:T(8,128)(2,1)} %copy-done.37), channel_id=1, source_target_pairs={{0,96},{32,0},{64,32},{96,64},{1,97},{33,1},{65,33},{97,65},{2,98}... | collective-permute-start | bytes 344072 | tf_op jit(solution)/shard_map/ppermute | solution.py:19
  171.7 11.2 %collective-permute-start.29 = (bf16[64,896]{1,0:T(8,128)(2,1)}, bf16[64,896]{1,0:T(8,128)(2,1)S(1)}, u32[]{:S(2)}, u32[]{:S(2)}) collective-permute-start(bf16[64,896]{1,0:T(8,128)(2,1)} %copy-done.36), channel_id=1, source_target_pairs={{0,64},{32,96},{64,0},{96,32},{1,65},{33,97},{65,1},{97,33},{2,66}... | collective-permute-start | bytes 344072 | tf_op jit(solution)/shard_map/ppermute | solution.py:19
  186.6 11.3 %collective-permute-start.34 = (bf16[3,64,896]{2,1,0:T(8,128)(2,1)S(1)}, bf16[3,64,896]{2,1,0:T(8,128)(2,1)S(1)}, u32[]{:S(2)}, u32[]{:S(2)}) collective-permute-start(bf16[3,64,896]{2,1,0:T(8,128)(2,1)S(1)} %pad_maximum_fusion.1.refs_0_), channel_id=1, source_target_pairs={{0,32},{32,64},{64,96},{96,0},{1,33},{33,65},{65,97},{97,1},{2,34}... | collective-permute-start | bytes 1032200 | tf_op jit(solution)/shard_map/ppermute | solution.py:19
  186.7 14.9 %collective-permute-start.35 = (bf16[3,64,896]{2,1,0:T(8,128)(2,1)S(1)}, bf16[3,64,896]{2,1,0:T(8,128)(2,1)S(1)}, u32[]{:S(2)}, u32[]{:S(2)}) collective-permute-start(bf16[3,64,896]{2,1,0:T(8,128)(2,1)S(1)} %pad_maximum_fusion.1.refs_0_), channel_id=1, source_target_pairs={{0,64},{32,96},{64,0},{96,32},{1,65},{33,97},{65,1},{97,33},{2,66}... | collective-permute-start | bytes 1032200 | tf_op jit(solution)/shard_map/ppermute | solution.py:19
  190.9 10.7 %collective-permute-start.36 = (bf16[3,64,896]{2,1,0:T(8,128)(2,1)S(1)}, bf16[3,64,896]{2,1,0:T(8,128)(2,1)S(1)}, u32[]{:S(2)}, u32[]{:S(2)}) collective-permute-start(bf16[3,64,896]{2,1,0:T(8,128)(2,1)S(1)} %pad_maximum_fusion.1.refs_0_), channel_id=1, source_target_pairs={{0,96},{32,0},{64,32},{96,64},{1,97},{33,1},{65,33},{97,65},{2,98}... | collective-permute-start | bytes 1032200 | tf_op jit(solution)/shard_map/ppermute | solution.py:19
  209.1 18.1 %all-to-all-start.1 = ((bf16[8,256,256]{2,1,0:T(8,128)(2,1)}), bf16[8,256,256]{2,1,0:T(8,128)(2,1)}, u32[]{:S(2)}, u32[]{:S(2)}) async-start(bf16[8,256,256]{2,1,0:T(8,128)(2,1)} %copy-done.15), calls=%async_computation.1 | async-start | bytes 2097152 | tf_op jit(solution)/shard_map/all_to_all | solution.py:331
  214.6 102.1 %reduce-scatter.2.cloned.1.call-start = ((), (), s32[]{:S(2)}) async-start(), calls=%async_computation.4 | async-start | bytes 1179648 | tf_op jit(solution)/shard_map/reduce_scatter | solution.py:462
  229.5 8.9 %collective-permute-start.37 = (bf16[256,256]{1,0:T(8,128)(2,1)S(1)}, bf16[256,256]{1,0:T(8,128)(2,1)S(1)}, u32[]{:S(2)}, u32[]{:S(2)}) collective-permute-start(bf16[256,256]{1,0:T(8,128)(2,1)S(1)} %add_convert_fusion.2.refs_0_), channel_id=1, source_target_pairs={{0,1},{1,2},{2,3},{3,4},{4,5},{5,6},{6,7},{7,0},{8,9},{9,10},{10,1... | collective-permute-start | bytes 393224 | tf_op jit(solution)/shard_map/ppermute | solution.py:19
  230.4 8.6 %collective-permute-start.38 = (bf16[256,256]{1,0:T(8,128)(2,1)S(1)}, bf16[256,256]{1,0:T(8,128)(2,1)S(1)}, u32[]{:S(2)}, u32[]{:S(2)}) collective-permute-start(bf16[256,256]{1,0:T(8,128)(2,1)S(1)} %add_convert_fusion.2.refs_0_), channel_id=1, source_target_pairs={{0,2},{1,3},{2,4},{3,5},{4,6},{5,7},{6,0},{7,1},{8,10},{9,11},{10,... | collective-permute-start | bytes 393224 | tf_op jit(solution)/shard_map/ppermute | solution.py:19
  232.8 12.3 %collective-permute-start.39 = (bf16[256,256]{1,0:T(8,128)(2,1)S(1)}, bf16[256,256]{1,0:T(8,128)(2,1)S(1)}, u32[]{:S(2)}, u32[]{:S(2)}) collective-permute-start(bf16[256,256]{1,0:T(8,128)(2,1)S(1)} %add_convert_fusion.2.refs_0_), channel_id=1, source_target_pairs={{0,3},{1,4},{2,5},{3,6},{4,7},{5,0},{6,1},{7,2},{8,11},{9,12},{10,... | collective-permute-start | bytes 393224 | tf_op jit(solution)/shard_map/ppermute | solution.py:19
  233.9 11.2 %collective-permute-start.40 = (bf16[256,256]{1,0:T(8,128)(2,1)S(1)}, bf16[256,256]{1,0:T(8,128)(2,1)S(1)}, u32[]{:S(2)}, u32[]{:S(2)}) collective-permute-start(bf16[256,256]{1,0:T(8,128)(2,1)S(1)} %add_convert_fusion.2.refs_0_), channel_id=1, source_target_pairs={{0,4},{1,5},{2,6},{3,7},{4,0},{5,1},{6,2},{7,3},{8,12},{9,13},{10,... | collective-permute-start | bytes 393224 | tf_op jit(solution)/shard_map/ppermute | solution.py:19
  235.3 9.7 %collective-permute-start.41 = (bf16[256,256]{1,0:T(8,128)(2,1)S(1)}, bf16[256,256]{1,0:T(8,128)(2,1)S(1)}, u32[]{:S(2)}, u32[]{:S(2)}) collective-permute-start(bf16[256,256]{1,0:T(8,128)(2,1)S(1)} %add_convert_fusion.2.refs_0_), channel_id=1, source_target_pairs={{0,5},{1,6},{2,7},{3,0},{4,1},{5,2},{6,3},{7,4},{8,13},{9,14},{10,... | collective-permute-start | bytes 393224 | tf_op jit(solution)/shard_map/ppermute | solution.py:19
  238.5 8.6 %collective-permute-start.42 = (bf16[256,256]{1,0:T(8,128)(2,1)S(1)}, bf16[256,256]{1,0:T(8,128)(2,1)S(1)}, u32[]{:S(2)}, u32[]{:S(2)}) collective-permute-start(bf16[256,256]{1,0:T(8,128)(2,1)S(1)} %add_convert_fusion.2.refs_0_), channel_id=1, source_target_pairs={{0,6},{1,7},{2,0},{3,1},{4,2},{5,3},{6,4},{7,5},{8,14},{9,15},{10,... | collective-permute-start | bytes 393224 | tf_op jit(solution)/shard_map/ppermute | solution.py:19
  250.0 12.1 %collective-permute-start.44 = (bf16[64,1792]{1,0:T(8,128)(2,1)S(1)}, bf16[64,1792]{1,0:T(8,128)(2,1)S(1)}, u32[]{:S(2)}, u32[]{:S(2)}) collective-permute-start(bf16[64,1792]{1,0:T(8,128)(2,1)S(1)} %get-tuple-element.150), channel_id=1, source_target_pairs={{0,32},{32,64},{64,96},{96,0},{1,33},{33,65},{65,97},{97,1},{2,34}... | collective-permute-start | bytes 688136 | tf_op jit(solution)/shard_map/ppermute | solution.py:19
  252.5 9.7 %collective-permute-start.45 = (bf16[64,1792]{1,0:T(8,128)(2,1)S(1)}, bf16[64,1792]{1,0:T(8,128)(2,1)S(1)}, u32[]{:S(2)}, u32[]{:S(2)}) collective-permute-start(bf16[64,1792]{1,0:T(8,128)(2,1)S(1)} %get-tuple-element.151), channel_id=1, source_target_pairs={{0,64},{32,96},{64,0},{96,32},{1,65},{33,97},{65,1},{97,33},{2,66}... | collective-permute-start | bytes 688136 | tf_op jit(solution)/shard_map/ppermute | solution.py:19
  263.4 14.9 %collective-permute-start.47 = (bf16[2,64,1792]{2,1,0:T(8,128)(2,1)}, bf16[2,64,1792]{2,1,0:T(8,128)(2,1)}, u32[]{:S(2)}, u32[]{:S(2)}) collective-permute-start(bf16[2,64,1792]{2,1,0:T(8,128)(2,1)} %pad_maximum_fusion.refs_0_), channel_id=1, source_target_pairs={{0,32},{32,64},{64,96},{96,0},{1,33},{33,65},{65,97},{97,1},{2,34}... | collective-permute-start | bytes 1376264 | tf_op jit(solution)/shard_map/ppermute | solution.py:19
  265.1 18.2 %collective-permute-start.48 = (bf16[2,64,1792]{2,1,0:T(8,128)(2,1)}, bf16[2,64,1792]{2,1,0:T(8,128)(2,1)}, u32[]{:S(2)}, u32[]{:S(2)}) collective-permute-start(bf16[2,64,1792]{2,1,0:T(8,128)(2,1)} %pad_maximum_fusion.refs_0_), channel_id=1, source_target_pairs={{0,64},{32,96},{64,0},{96,32},{1,65},{33,97},{65,1},{97,33},{2,66}... | collective-permute-start | bytes 1376264 | tf_op jit(solution)/shard_map/ppermute | solution.py:19
  267.1 16.4 %collective-permute-start.49 = (bf16[2,64,1792]{2,1,0:T(8,128)(2,1)}, bf16[2,64,1792]{2,1,0:T(8,128)(2,1)}, u32[]{:S(2)}, u32[]{:S(2)}) collective-permute-start(bf16[2,64,1792]{2,1,0:T(8,128)(2,1)} %pad_maximum_fusion.refs_0_), channel_id=1, source_target_pairs={{0,96},{32,0},{64,32},{96,64},{1,97},{33,1},{65,33},{97,65},{2,98}... | collective-permute-start | bytes 1376264 | tf_op jit(solution)/shard_map/ppermute | solution.py:19
  (48 other events, 304.6 us)
Sparse Core Ops, SparseCore 0:
  55.0 64.4 all-gather.2
  267.9 44.2 reduce-scatter.1
where the time goes:
time: 327 us; the launch traced here: 325 us
  starting transfers between devices  103 us (31%)
  waiting for transfers between devices  89.4 us (27%)
  Pallas kernels  41.9 us (13%)
  local copies, waits for them, and re-layouts  37.2 us (11%)
  blocking collectives  26.9 us (8%)
  between operations  15.9 us (5%)
  other arithmetic  10.8 us (3%)
    ppermute x42, starting transfers between devices, send(): lax.ppermute(p, axis, ring(n, r))  69.4 us
    ppermute x42, waiting for transfers between devices, send(): lax.ppermute(p, axis, ring(n, r))  49.5 us
    pallas_call x9, Pallas kernels, call(): pl.pallas_call(kernel, in_specs=[SM] + [VM] * len(operands), out_specs=[V...  39 us
    unnamed x84, local copies, waits for them, and re-layouts  37.2 us
    all_to_all x1, blocking collectives, add_over_tensor(): lax.all_to_all(parts, 'tensor', split_axis=0, concat_axis=0, tiled=True)  26.9 us
    ppermute x4, waiting for transfers between devices, hand_out(): return lax.ppermute(piece, ('dp', 'tensor'), perm)  26.7 us
    all_to_all x2, starting transfers between devices, add_over_tensor(): lax.all_to_all(parts, 'tensor', split_axis=0, concat_axis=0, tiled=True)  18.5 us
    ppermute x4, starting transfers between devices, hand_out(): return lax.ppermute(piece, ('dp', 'tensor'), perm)  13.7 us
  transfers between devices with their start and end apart: 54, of which 23 were waited for; matrix products, arithmetic and copies ran while one was open for 2% of the time, Pallas kernels for 9%

commit v1 on v0

--- a/solution.py
+++ b/solution.py
@@ -188,13 +188,13 @@
             at = pl.multiple_of(narrow_owner(j, mix) * width, width)
             out[:, pl.ds(at, width)] = lax.dot_general(
                 lhs[...], w[2], NT, preferred_element_type=F32
-            ).astype(BF)
+            )
 
     return call(
         kernel,
         idx,
         (*chunks, *weights),
-        [((tokens, feats), BF)],
+        [((tokens, feats), F32)],
         [pltpu.VMEM((tokens, units), BF)],
         2 * tokens * feats * units,
         2 * feats * units,
@@ -460,7 +460,7 @@
 
     received = send(parts, "section", 4)
     out_sum = lax.psum_scatter(after(out_part, own), "tensor", scatter_dimension=0, tiled=True)
-    outputs = (mid_rows.astype(F32) + out_sum.astype(F32)).astype(BF)
+    outputs = (mid_rows.astype(F32) + out_sum).astype(BF)
 
     gate_2, = into_vmem(after(gate_wide, own))
     dhid_a = add_up(own, after(received, gate_2))

time: 327 us -> 324 us (level)
    unnamed x84 -> x72, local copies, waits for them, and re-layouts: 37.2 us -> 34.6 us
  transfers between devices with their start and end apart: 54 -> 54, of which waited for: 23 -> 22; matrix products, arithmetic and copies ran while one was open for 2% -> 2% of each run, Pallas kernels for 9% -> 9%
where the time goes in v1:
time: 324 us; the launch traced here: 323 us
  starting transfers between devices  104 us (32%)
  waiting for transfers between devices  88.9 us (27%)
  Pallas kernels  42.6 us (13%)
  local copies, waits for them, and re-layouts  34.6 us (11%)
  blocking collectives  27.1 us (8%)
  between operations  15.9 us (5%)
  other arithmetic  10 us (3%)
    ppermute x42, starting transfers between devices, send(): lax.ppermute(p, axis, ring(n, r))  69.1 us
    ppermute x42, waiting for transfers between devices, send(): lax.ppermute(p, axis, ring(n, r))  52.2 us
    pallas_call x9, Pallas kernels, call(): pl.pallas_call(kernel, in_specs=[SM] + [VM] * len(operands), out_specs=[V...  39.7 us
    unnamed x72, local copies, waits for them, and re-layouts  34.6 us
    all_to_all x1, blocking collectives, add_over_tensor(): lax.all_to_all(parts, 'tensor', split_axis=0, concat_axis=0, tiled=True)  27.1 us
    ppermute x4, waiting for transfers between devices, hand_out(): return lax.ppermute(piece, ('dp', 'tensor'), perm)  24 us
    all_to_all x2, starting transfers between devices, add_over_tensor(): lax.all_to_all(parts, 'tensor', split_axis=0, concat_axis=0, tiled=True)  19.8 us
    ppermute x4, starting transfers between devices, hand_out(): return lax.ppermute(piece, ('dp', 'tensor'), perm)  13.8 us
  transfers between devices with their start and end apart: 54, of which 22 were waited for; matrix products, arithmetic and copies ran while one was open for 2% of the time, Pallas kernels for 9%

profile of v1, /device:TPU:0, one launch (start us, length us, event | category | flops | bytes accessed | tf_op | source)
XLA Modules:
  0.0 322.9 jit_solution(6814478682563096039)
XLA Ops:
  8.9 2.9 collective-permute-start.1
  11.8 2.3 collective-permute-start.2
  16.6 3.2 collective-permute-start.5
  23.4 2.4 shard_map.113
  28.9 5.6 %collective-permute-start.11 = (bf16[3,256,896]{2,1,0:T(8,128)(2,1)}, bf16[3,256,896]{2,1,0:T(8,128)(2,1)S(1)}, u32[]{:S(2)}, u32[]{:S(2)}) collective-permute-start(bf16[3,256,896]{2,1,0:T(8,128)(2,1)} %get-tuple-element.108), channel_id=1, source_target_pairs={{0,17},{1,25},{2,16},{3,24},{4,1},{5,9},{6,0},{7,8},{8,21},{9,29},... | collective-permute-start | bytes 4128776 | tf_op jit(solution)/shard_map/ppermute | solution.py:385
  34.5 3.1 copy-done.2
  37.5 3.1 copy-done.4
  41.6 6.7 %shard_map.115 = (f32[2,64,1792]{2,1,0:T(8,128)S(1)}, bf16[2,64,1792]{2,1,0:T(8,128)(2,1)}, bf16[2,64,1792]{2,1,0:T(8,128)(2,1)}, bf16[2,64,1792]{2,1,0:T(8,128)(2,1)}, bf16[32,2048]{1,0:T(8,128)(2,1)}) custom-call(s32[3]{0:T(128)S(1)} %pad_add_fusion.idx_ref, bf16[256,256]{1,0:T(8,128)(2,1)S(1)} %bitcast.89, ...), custom_call_target="tpu_custom_call" | custom-call | flops 3758096384 | bytes 14680064 | tf_op jit(solution)/shard_map/pallas_call | solution.py:63
  49.3 4.0 %collective-permute-start.9 = (bf16[2,64,1792]{2,1,0:T(8,128)(2,1)}, bf16[2,64,1792]{2,1,0:T(8,128)(2,1)S(1)}, u32[]{:S(2)}, u32[]{:S(2)}) collective-permute-start(bf16[2,64,1792]{2,1,0:T(8,128)(2,1)} %get-tuple-element.99), channel_id=1, source_target_pairs={{0,96},{32,0},{64,32},{96,64},{1,97},{33,1},{65,33},{97,65},{2,98}... | collective-permute-start | bytes 1376264 | tf_op jit(solution)/shard_map/ppermute | solution.py:19
  55.3 13.3 %collective-permute-done.11.refs_4_.refs_11_.refs_7_ = bf16[3,256,896]{2,1,0:T(8,128)(2,1)S(1)} collective-permute-done((bf16[3,256,896]{2,1,0:T(8,128)(2,1)}, bf16[3,256,896]{2,1,0:T(8,128)(2,1)S(1)}, u32[]{:S(2)}, u32[]{:S(2)}) %collective-permute-start.11) | collective-permute-done | bytes 1376288 | tf_op jit(solution)/shard_map/ppermute | solution.py:385
  68.6 6.2 %collective-permute-start.16 = (bf16[3,256,896]{2,1,0:T(8,128)(2,1)}, bf16[3,256,896]{2,1,0:T(8,128)(2,1)}, u32[]{:S(2)}, u32[]{:S(2)}) collective-permute-start(bf16[3,256,896]{2,1,0:T(8,128)(2,1)} %get-tuple-element.109), channel_id=1, source_target_pairs={{0,16},{1,24},{2,17},{3,25},{4,0},{5,8},{6,1},{7,9},{8,20},{9,28},... | collective-permute-start | bytes 4128776 | tf_op jit(solution)/shard_map/ppermute | solution.py:385
  78.8 3.9 %collective-permute-start.13 = (bf16[64,1792]{1,0:T(8,128)(2,1)S(1)}, bf16[64,1792]{1,0:T(8,128)(2,1)S(1)}, u32[]{:S(2)}, u32[]{:S(2)}) collective-permute-start(bf16[64,1792]{1,0:T(8,128)(2,1)S(1)} %multiply_convert_fusion.2.refs_0_), channel_id=1, source_target_pairs={{0,64},{32,96},{64,0},{96,32},{1,65},{33,97},{65,1},{97,33},{2,66}... | collective-permute-start | bytes 688136 | tf_op jit(solution)/shard_map/ppermute | solution.py:19
  83.6 3.1 copy-done
  87.2 4.3 %collective-permute-done.12.refs_1_ = bf16[64,1792]{1,0:T(8,128)(2,1)S(1)} collective-permute-done((bf16[64,1792]{1,0:T(8,128)(2,1)S(1)}, bf16[64,1792]{1,0:T(8,128)(2,1)S(1)}, u32[]{:S(2)}, u32[]{:S(2)}) %collective-permute-start.12) | collective-permute-done | bytes 229408 | tf_op jit(solution)/shard_map/ppermute | solution.py:19
  92.1 2.6 shard_map.117
  95.8 10.7 %collective-permute-done.15.refs_2_.refs_9_.refs_5_ = bf16[3,256,896]{2,1,0:T(8,128)(2,1)} collective-permute-done((bf16[3,256,896]{2,1,0:T(8,128)(2,1)}, bf16[3,256,896]{2,1,0:T(8,128)(2,1)}, u32[]{:S(2)}, u32[]{:S(2)}) %collective-permute-start.15) | collective-permute-done | bytes 1376288 | tf_op jit(solution)/shard_map/ppermute | solution.py:385
  106.5 13.4 %all-to-all-start = ((bf16[8,256,256]{2,1,0:T(8,128)(2,1)}), bf16[8,256,256]{2,1,0:T(8,128)(2,1)}, u32[]{:S(2)}, u32[]{:S(2)}) async-start(bf16[8,256,256]{2,1,0:T(8,128)(2,1)} %copy-done.12), calls=%async_computation | async-start | bytes 2097152 | tf_op jit(solution)/shard_map/all_to_all | solution.py:331
  120.4 11.2 %all-to-all-done = bf16[8,256,256]{2,1,0:T(8,128)(2,1)} async-done(((bf16[8,256,256]{2,1,0:T(8,128)(2,1)}), bf16[8,256,256]{2,1,0:T(8,128)(2,1)}, u32[]{:S(2)}, u32[]{:S(2)}) %all-to-all-start) | async-done | bytes 1048608 | tf_op jit(solution)/shard_map/all_to_all | solution.py:331
  134.0 2.5 collective-permute-start.18
  137.9 6.0 %collective-permute-done.17.refs_1_ = bf16[256,256]{1,0:T(8,128)(2,1)S(1)} collective-permute-done((bf16[256,256]{1,0:T(8,128)(2,1)S(1)}, bf16[256,256]{1,0:T(8,128)(2,1)S(1)}, u32[]{:S(2)}, u32[]{:S(2)}) %collective-permute-start.17) | collective-permute-done | bytes 131104 | tf_op jit(solution)/shard_map/ppermute | solution.py:19
  144.3 2.9 collective-permute-start.21
  151.2 4.0 %shard_map.118 = (f32[64,896]{1,0:T(8,128)S(1)}, bf16[64,896]{1,0:T(8,128)(2,1)S(1)}, bf16[64,896]{1,0:T(8,128)(2,1)S(1)}, bf16[64,896]{1,0:T(8,128)(2,1)S(1)}, bf16[256,256]{1,0:T(8,128)(2,1)S(1)}) custom-call(s32[3]{0:T(128)S(1)} %pad_add_fusion.idx_ref, bf16[256,2048]{1,0:T(8,128)(2,1)S(1)} %bitcast.81, ...), custom_call_target="tpu_custom_call" | custom-call | flops 939524096 | bytes 3670016 | tf_op jit(solution)/shard_map/pallas_call | solution.py:63
  156.0 6.3 %shard_map.119 = (f32[2,64,896]{2,1,0:T(8,128)S(1)}, bf16[2,64,896]{2,1,0:T(8,128)(2,1)}, bf16[2,64,896]{2,1,0:T(8,128)(2,1)}, bf16[2,64,896]{2,1,0:T(8,128)(2,1)}, bf16[32,2048]{1,0:T(8,128)(2,1)S(1)}) custom-call(s32[3]{0:T(128)S(1)} %pad_add_fusion.idx_ref, bf16[256,256]{1,0:T(8,128)(2,1)S(1)} %add_convert_fusion.3.refs_0_, ...), custom_call_target="tpu_custom_call" | custom-call | flops 1879048192 | bytes 7340032 | tf_op jit(solution)/shard_map/pallas_call | solution.py:63
  162.9 5.3 %collective-permute-start.33 = (bf16[2,64,896]{2,1,0:T(8,128)(2,1)}, bf16[2,64,896]{2,1,0:T(8,128)(2,1)}, u32[]{:S(2)}, u32[]{:S(2)}) collective-permute-start(bf16[2,64,896]{2,1,0:T(8,128)(2,1)} %get-tuple-element.133), channel_id=1, source_target_pairs={{0,96},{32,0},{64,32},{96,64},{1,97},{33,1},{65,33},{97,65},{2,98}... | collective-permute-start | bytes 688136 | tf_op jit(solution)/shard_map/ppermute | solution.py:19
  169.8 2.4 collective-permute-start.30
  172.2 2.3 collective-permute-start.29
  174.5 5.4 %collective-permute-done.33 = bf16[2,64,896]{2,1,0:T(8,128)(2,1)} collective-permute-done((bf16[2,64,896]{2,1,0:T(8,128)(2,1)}, bf16[2,64,896]{2,1,0:T(8,128)(2,1)}, u32[]{:S(2)}, u32[]{:S(2)}) %collective-permute-start.33) | collective-permute-done | bytes 229408 | tf_op jit(solution)/shard_map/ppermute | solution.py:19
  183.6 3.3 %collective-permute-done.28 = bf16[64,896]{1,0:T(8,128)(2,1)S(1)} collective-permute-done((bf16[64,896]{1,0:T(8,128)(2,1)}, bf16[64,896]{1,0:T(8,128)(2,1)S(1)}, u32[]{:S(2)}, u32[]{:S(2)}) %collective-permute-start.28) | collective-permute-done | bytes 114720 | tf_op jit(solution)/shard_map/ppermute | solution.py:19
  187.2 4.4 %collective-permute-start.35 = (bf16[3,64,896]{2,1,0:T(8,128)(2,1)S(1)}, bf16[3,64,896]{2,1,0:T(8,128)(2,1)S(1)}, u32[]{:S(2)}, u32[]{:S(2)}) collective-permute-start(bf16[3,64,896]{2,1,0:T(8,128)(2,1)S(1)} %pad_maximum_fusion.1.refs_0_), channel_id=1, source_target_pairs={{0,64},{32,96},{64,0},{96,32},{1,65},{33,97},{65,1},{97,33},{2,66}... | collective-permute-start | bytes 1032200 | tf_op jit(solution)/shard_map/ppermute | solution.py:19
  191.9 6.3 %collective-permute-done.34.refs_1_ = bf16[3,64,896]{2,1,0:T(8,128)(2,1)S(1)} collective-permute-done((bf16[3,64,896]{2,1,0:T(8,128)(2,1)S(1)}, bf16[3,64,896]{2,1,0:T(8,128)(2,1)S(1)}, u32[]{:S(2)}, u32[]{:S(2)}) %collective-permute-start.34) | collective-permute-done | bytes 344096 | tf_op jit(solution)/shard_map/ppermute | solution.py:19
  198.2 3.7 %collective-permute-done.35.refs_2_ = bf16[3,64,896]{2,1,0:T(8,128)(2,1)S(1)} collective-permute-done((bf16[3,64,896]{2,1,0:T(8,128)(2,1)S(1)}, bf16[3,64,896]{2,1,0:T(8,128)(2,1)S(1)}, u32[]{:S(2)}, u32[]{:S(2)}) %collective-permute-start.35) | collective-permute-done | bytes 344096 | tf_op jit(solution)/shard_map/ppermute | solution.py:19
  201.9 5.0 %shard_map.120 = bf16[8,256,256]{2,1,0:T(8,128)(2,1)S(1)} custom-call(s32[3]{0:T(128)S(1)} %pad_add_fusion.idx_ref, bf16[3,64,896]{2,1,0:T(8,128)(2,1)S(1)} %pad_maximum_fusion.1.refs_0_, bf16[3,64,896]{2,1,0:T(8,128)(2,1)S(1)} %collective-permute-done.34.refs_1_, bf16[3,64,896]{2,1,0:T(8,128)(2,1)S(1)} %collective-permute-done.35.refs_2_, ...), custom_call_target="tpu_custom_call" | custom-call | flops 1879048192 | bytes 7340032 | tf_op jit(solution)/shard_map/pallas_call | solution.py:63
  209.4 6.4 %all-to-all-start.1 = ((bf16[8,256,256]{2,1,0:T(8,128)(2,1)}), bf16[8,256,256]{2,1,0:T(8,128)(2,1)}, u32[]{:S(2)}, u32[]{:S(2)}) async-start(bf16[8,256,256]{2,1,0:T(8,128)(2,1)} %copy-done.13), calls=%async_computation.1 | async-start | bytes 2097152 | tf_op jit(solution)/shard_map/all_to_all | solution.py:331
  220.4 5.3 %shard_map.121 = f32[256,2048]{1,0:T(8,128)} custom-call(s32[3]{0:T(128)S(1)} %pad_add_fusion.idx_ref, bf16[3,64,896]{2,1,0:T(8,128)(2,1)S(1)} %pad_maximum_fusion.1.refs_0_, bf16[3,64,896]{2,1,0:T(8,128)(2,1)S(1)} %collective-permute-done.34.refs_1_, bf16[3,64,896]{2,1,0:T(8,128)(2,1)S(1)} %copy-done.15, bf16[3,64,896]{2,1,0:T(8,128)(2,1)S(1)} %copy-done.17, ...), custom_call_target="tpu_custom_call" | custom-call | flops 939524096 | bytes 3670016 | tf_op jit(solution)/shard_map/pallas_call | solution.py:63
  230.5 2.6 collective-permute-start.38
  233.1 2.1 collective-permute-start.39
  239.4 2.4 collective-permute-start.43
  241.8 3.1 copy-done.1
  247.1 2.9 shard_map.123
  251.3 4.0 %collective-permute-start.45 = (bf16[64,1792]{1,0:T(8,128)(2,1)S(1)}, bf16[64,1792]{1,0:T(8,128)(2,1)S(1)}, u32[]{:S(2)}, u32[]{:S(2)}) collective-permute-start(bf16[64,1792]{1,0:T(8,128)(2,1)S(1)} %get-tuple-element.151), channel_id=1, source_target_pairs={{0,64},{32,96},{64,0},{96,32},{1,65},{33,97},{65,1},{97,33},{2,66}... | collective-permute-start | bytes 688136 | tf_op jit(solution)/shard_map/ppermute | solution.py:19
  255.3 3.1 copy-done.3
  259.6 2.5 collective-permute-done.45
  262.7 3.6 %collective-permute-start.48 = (bf16[2,64,1792]{2,1,0:T(8,128)(2,1)S(1)}, bf16[2,64,1792]{2,1,0:T(8,128)(2,1)S(1)}, u32[]{:S(2)}, u32[]{:S(2)}) collective-permute-start(bf16[2,64,1792]{2,1,0:T(8,128)(2,1)S(1)} %pad_maximum_fusion.refs_0_), channel_id=1, source_target_pairs={{0,64},{32,96},{64,0},{96,32},{1,65},{33,97},{65,1},{97,33},{2,66}... | collective-permute-start | bytes 1376264 | tf_op jit(solution)/shard_map/ppermute | solution.py:19
  266.6 3.2 copy-done.5
  270.3 6.8 %collective-permute-done.47.refs_1_ = bf16[2,64,1792]{2,1,0:T(8,128)(2,1)S(1)} collective-permute-done((bf16[2,64,1792]{2,1,0:T(8,128)(2,1)S(1)}, bf16[2,64,1792]{2,1,0:T(8,128)(2,1)S(1)}, u32[]{:S(2)}, u32[]{:S(2)}) %collective-permute-start.47) | collective-permute-done | bytes 458784 | tf_op jit(solution)/shard_map/ppermute | solution.py:19
  277.1 4.9 %collective-permute-done.48.refs_2_ = bf16[2,64,1792]{2,1,0:T(8,128)(2,1)S(1)} collective-permute-done((bf16[2,64,1792]{2,1,0:T(8,128)(2,1)S(1)}, bf16[2,64,1792]{2,1,0:T(8,128)(2,1)S(1)}, u32[]{:S(2)}, u32[]{:S(2)}) %collective-permute-start.48) | collective-permute-done | bytes 458784 | tf_op jit(solution)/shard_map/ppermute | solution.py:19
  282.0 4.5 %shard_map.126 = bf16[8,256,256]{2,1,0:T(8,128)(2,1)S(1)} custom-call(s32[3]{0:T(128)S(1)} %pad_add_fusion.idx_ref, bf16[2,64,1792]{2,1,0:T(8,128)(2,1)S(1)} %pad_maximum_fusion.refs_0_, bf16[2,64,1792]{2,1,0:T(8,128)(2,1)S(1)} %collective-permute-done.47.refs_1_, bf16[2,64,1792]{2,1,0:T(8,128)(2,1)S(1)} %collective-permute-done.48.refs_2_, ...), custom_call_target="tpu_custom_call" | custom-call | flops 3758096384 | bytes 14680064 | tf_op jit(solution)/shard_map/pallas_call | solution.py:63
  286.6 27.1 %all_to_all.15 = bf16[8,256,256]{2,1,0:T(8,128)(2,1)S(1)} all-to-all(bf16[8,256,256]{2,1,0:T(8,128)(2,1)S(1)} %shard_map.126), channel_id=1, replica_groups=mesh['section'=4,'dp'=4,'tensor'=8] {'tensor'}, dimensions={0} | all-to-all | bytes 2097152 | tf_op jit(solution)/shard_map/all_to_all | solution.py:331
  (168 shorter events, 61.1 us)
Async XLA Ops:
  7.2 125.8 %all-gather.3.cloned.1.call-start = ((), (), s32[]{:S(2)}) async-start(), calls=%async_computation.5 | async-start | bytes 1179648 | tf_op jit(solution)/shard_map/all_gather | solution.py:423
  7.2 9.4 %collective-permute-start = (bf16[256,256]{1,0:T(8,128)(2,1)}, bf16[256,256]{1,0:T(8,128)(2,1)S(1)}, u32[]{:S(2)}, u32[]{:S(2)}) collective-permute-start(bf16[256,256]{1,0:T(8,128)(2,1)} %bitcast.82), channel_id=1, source_target_pairs={{0,1},{1,2},{2,3},{3,4},{4,5},{5,6},{6,7},{7,0},{8,9},{9,10},{10,1... | collective-permute-start | bytes 393224 | tf_op jit(solution)/shard_map/ppermute | solution.py:19
  8.9 10.8 %collective-permute-start.1 = (bf16[256,256]{1,0:T(8,128)(2,1)}, bf16[256,256]{1,0:T(8,128)(2,1)S(1)}, u32[]{:S(2)}, u32[]{:S(2)}) collective-permute-start(bf16[256,256]{1,0:T(8,128)(2,1)} %bitcast.83), channel_id=1, source_target_pairs={{0,2},{1,3},{2,4},{3,5},{4,6},{5,7},{6,0},{7,1},{8,10},{9,11},{10,... | collective-permute-start | bytes 393224 | tf_op jit(solution)/shard_map/ppermute | solution.py:19
  11.8 13.9 %collective-permute-start.2 = (bf16[256,256]{1,0:T(8,128)(2,1)}, bf16[256,256]{1,0:T(8,128)(2,1)S(1)}, u32[]{:S(2)}, u32[]{:S(2)}) collective-permute-start(bf16[256,256]{1,0:T(8,128)(2,1)} %bitcast.84), channel_id=1, source_target_pairs={{0,3},{1,4},{2,5},{3,6},{4,7},{5,0},{6,1},{7,2},{8,11},{9,12},{10,... | collective-permute-start | bytes 393224 | tf_op jit(solution)/shard_map/ppermute | solution.py:19
  14.1 11.6 %collective-permute-start.3 = (bf16[256,256]{1,0:T(8,128)(2,1)}, bf16[256,256]{1,0:T(8,128)(2,1)S(1)}, u32[]{:S(2)}, u32[]{:S(2)}) collective-permute-start(bf16[256,256]{1,0:T(8,128)(2,1)} %bitcast.85), channel_id=1, source_target_pairs={{0,4},{1,5},{2,6},{3,7},{4,0},{5,1},{6,2},{7,3},{8,12},{9,13},{10,... | collective-permute-start | bytes 393224 | tf_op jit(solution)/shard_map/ppermute | solution.py:19
  14.7 11.1 %collective-permute-start.4 = (bf16[256,256]{1,0:T(8,128)(2,1)}, bf16[256,256]{1,0:T(8,128)(2,1)S(1)}, u32[]{:S(2)}, u32[]{:S(2)}) collective-permute-start(bf16[256,256]{1,0:T(8,128)(2,1)} %bitcast.86), channel_id=1, source_target_pairs={{0,5},{1,6},{2,7},{3,0},{4,1},{5,2},{6,3},{7,4},{8,13},{9,14},{10,... | collective-permute-start | bytes 393224 | tf_op jit(solution)/shard_map/ppermute | solution.py:19
  16.6 9.2 %collective-permute-start.5 = (bf16[256,256]{1,0:T(8,128)(2,1)}, bf16[256,256]{1,0:T(8,128)(2,1)S(1)}, u32[]{:S(2)}, u32[]{:S(2)}) collective-permute-start(bf16[256,256]{1,0:T(8,128)(2,1)} %bitcast.87), channel_id=1, source_target_pairs={{0,6},{1,7},{2,0},{3,1},{4,2},{5,3},{6,4},{7,5},{8,14},{9,15},{10,... | collective-permute-start | bytes 393224 | tf_op jit(solution)/shard_map/ppermute | solution.py:19
  26.9 28.4 %collective-permute-start.10 = (bf16[3,256,896]{2,1,0:T(8,128)(2,1)}, bf16[3,256,896]{2,1,0:T(8,128)(2,1)S(1)}, u32[]{:S(2)}, u32[]{:S(2)}) collective-permute-start(bf16[3,256,896]{2,1,0:T(8,128)(2,1)} %get-tuple-element.109), channel_id=1, source_target_pairs={{0,0},{1,8},{2,1},{3,9},{4,16},{5,24},{6,17},{7,25},{8,4},{9,12},{... | collective-permute-start | bytes 4128776 | tf_op jit(solution)/shard_map/ppermute | solution.py:385
  28.9 39.8 %collective-permute-start.11 = (bf16[3,256,896]{2,1,0:T(8,128)(2,1)}, bf16[3,256,896]{2,1,0:T(8,128)(2,1)S(1)}, u32[]{:S(2)}, u32[]{:S(2)}) collective-permute-start(bf16[3,256,896]{2,1,0:T(8,128)(2,1)} %get-tuple-element.108), channel_id=1, source_target_pairs={{0,17},{1,25},{2,16},{3,24},{4,1},{5,9},{6,0},{7,8},{8,21},{9,29},... | collective-permute-start | bytes 4128776 | tf_op jit(solution)/shard_map/ppermute | solution.py:385
  49.3 25.6 %collective-permute-start.9 = (bf16[2,64,1792]{2,1,0:T(8,128)(2,1)}, bf16[2,64,1792]{2,1,0:T(8,128)(2,1)S(1)}, u32[]{:S(2)}, u32[]{:S(2)}) collective-permute-start(bf16[2,64,1792]{2,1,0:T(8,128)(2,1)} %get-tuple-element.99), channel_id=1, source_target_pairs={{0,96},{32,0},{64,32},{96,64},{1,97},{33,1},{65,33},{97,65},{2,98}... | collective-permute-start | bytes 1376264 | tf_op jit(solution)/shard_map/ppermute | solution.py:19
  53.3 21.5 %collective-permute-start.8 = (bf16[2,64,1792]{2,1,0:T(8,128)(2,1)}, bf16[2,64,1792]{2,1,0:T(8,128)(2,1)}, u32[]{:S(2)}, u32[]{:S(2)}) collective-permute-start(bf16[2,64,1792]{2,1,0:T(8,128)(2,1)} %get-tuple-element.98), channel_id=1, source_target_pairs={{0,64},{32,96},{64,0},{96,32},{1,65},{33,97},{65,1},{97,33},{2,66}... | collective-permute-start | bytes 1376264 | tf_op jit(solution)/shard_map/ppermute | solution.py:19
  53.4 23.0 %collective-permute-start.7 = (bf16[2,64,1792]{2,1,0:T(8,128)(2,1)}, bf16[2,64,1792]{2,1,0:T(8,128)(2,1)}, u32[]{:S(2)}, u32[]{:S(2)}) collective-permute-start(bf16[2,64,1792]{2,1,0:T(8,128)(2,1)} %get-tuple-element.97), channel_id=1, source_target_pairs={{0,32},{32,64},{64,96},{96,0},{1,33},{33,65},{65,97},{97,1},{2,34}... | collective-permute-start | bytes 1376264 | tf_op jit(solution)/shard_map/ppermute | solution.py:19
  68.6 37.9 %collective-permute-start.15 = (bf16[3,256,896]{2,1,0:T(8,128)(2,1)}, bf16[3,256,896]{2,1,0:T(8,128)(2,1)}, u32[]{:S(2)}, u32[]{:S(2)}) collective-permute-start(bf16[3,256,896]{2,1,0:T(8,128)(2,1)} %get-tuple-element.108), channel_id=1, source_target_pairs={{0,1},{1,9},{2,0},{3,8},{4,17},{5,25},{6,16},{7,24},{8,5},{9,13},{... | collective-permute-start | bytes 4128776 | tf_op jit(solution)/shard_map/ppermute | solution.py:385
  68.6 37.9 %collective-permute-start.16 = (bf16[3,256,896]{2,1,0:T(8,128)(2,1)}, bf16[3,256,896]{2,1,0:T(8,128)(2,1)}, u32[]{:S(2)}, u32[]{:S(2)}) collective-permute-start(bf16[3,256,896]{2,1,0:T(8,128)(2,1)} %get-tuple-element.109), channel_id=1, source_target_pairs={{0,16},{1,24},{2,17},{3,25},{4,0},{5,8},{6,1},{7,9},{8,20},{9,28},... | collective-permute-start | bytes 4128776 | tf_op jit(solution)/shard_map/ppermute | solution.py:385
  78.1 13.4 %collective-permute-start.12 = (bf16[64,1792]{1,0:T(8,128)(2,1)S(1)}, bf16[64,1792]{1,0:T(8,128)(2,1)S(1)}, u32[]{:S(2)}, u32[]{:S(2)}) collective-permute-start(bf16[64,1792]{1,0:T(8,128)(2,1)S(1)} %multiply_convert_fusion.2.refs_0_), channel_id=1, source_target_pairs={{0,32},{32,64},{64,96},{96,0},{1,33},{33,65},{65,97},{97,1},{2,34}... | collective-permute-start | bytes 688136 | tf_op jit(solution)/shard_map/ppermute | solution.py:19
  78.8 12.7 %collective-permute-start.13 = (bf16[64,1792]{1,0:T(8,128)(2,1)S(1)}, bf16[64,1792]{1,0:T(8,128)(2,1)S(1)}, u32[]{:S(2)}, u32[]{:S(2)}) collective-permute-start(bf16[64,1792]{1,0:T(8,128)(2,1)S(1)} %multiply_convert_fusion.2.refs_0_), channel_id=1, source_target_pairs={{0,64},{32,96},{64,0},{96,32},{1,65},{33,97},{65,1},{97,33},{2,66}... | collective-permute-start | bytes 688136 | tf_op jit(solution)/shard_map/ppermute | solution.py:19
  82.7 9.4 %collective-permute-start.14 = (bf16[64,1792]{1,0:T(8,128)(2,1)S(1)}, bf16[64,1792]{1,0:T(8,128)(2,1)S(1)}, u32[]{:S(2)}, u32[]{:S(2)}) collective-permute-start(bf16[64,1792]{1,0:T(8,128)(2,1)S(1)} %multiply_convert_fusion.2.refs_0_), channel_id=1, source_target_pairs={{0,96},{32,0},{64,32},{96,64},{1,97},{33,1},{65,33},{97,65},{2,98}... | collective-permute-start | bytes 688136 | tf_op jit(solution)/shard_map/ppermute | solution.py:19
  106.5 25.1 %all-to-all-start = ((bf16[8,256,256]{2,1,0:T(8,128)(2,1)}), bf16[8,256,256]{2,1,0:T(8,128)(2,1)}, u32[]{:S(2)}, u32[]{:S(2)}) async-start(bf16[8,256,256]{2,1,0:T(8,128)(2,1)} %copy-done.12), calls=%async_computation | async-start | bytes 2097152 | tf_op jit(solution)/shard_map/all_to_all | solution.py:331
  119.9 14.2 %collective-permute-start.24 = (bf16[3,256,896]{2,1,0:T(8,128)(2,1)S(1)}, bf16[3,256,896]{2,1,0:T(8,128)(2,1)}, u32[]{:S(2)}, u32[]{:S(2)}) collective-permute-start(bf16[3,256,896]{2,1,0:T(8,128)(2,1)S(1)} %collective-permute-done.10.refs_1_.refs_8_.refs_4_), channel_id=1, source_target_pairs={{0,8},{8,0},{16,24},{24,16},{1,9},{9,1},{17,25},{25,17},{2,10},{10... | collective-permute-start | bytes 4128776 | tf_op jit(solution)/shard_map/ppermute | solution.py:389
  119.9 16.6 %collective-permute-start.27 = (bf16[3,256,896]{2,1,0:T(8,128)(2,1)S(1)}, bf16[3,256,896]{2,1,0:T(8,128)(2,1)}, u32[]{:S(2)}, u32[]{:S(2)}) collective-permute-start(bf16[3,256,896]{2,1,0:T(8,128)(2,1)S(1)} %collective-permute-done.11.refs_4_.refs_11_.refs_7_), channel_id=1, source_target_pairs={{0,8},{8,0},{16,24},{24,16},{1,9},{9,1},{17,25},{25,17},{2,10},{10... | collective-permute-start | bytes 4128776 | tf_op jit(solution)/shard_map/ppermute | solution.py:389
  133.0 14.2 %collective-permute-start.25 = (bf16[3,256,896]{2,1,0:T(8,128)(2,1)}, bf16[3,256,896]{2,1,0:T(8,128)(2,1)S(1)}, u32[]{:S(2)}, u32[]{:S(2)}) collective-permute-start(bf16[3,256,896]{2,1,0:T(8,128)(2,1)} %collective-permute-done.15.refs_2_.refs_9_.refs_5_), channel_id=1, source_target_pairs={{0,8},{8,0},{16,24},{24,16},{1,9},{9,1},{17,25},{25,17},{2,10},{10... | collective-permute-start | bytes 4128776 | tf_op jit(solution)/shard_map/ppermute | solution.py:389
  133.1 16.0 %collective-permute-start.26 = (bf16[3,256,896]{2,1,0:T(8,128)(2,1)}, bf16[3,256,896]{2,1,0:T(8,128)(2,1)S(1)}, u32[]{:S(2)}, u32[]{:S(2)}) collective-permute-start(bf16[3,256,896]{2,1,0:T(8,128)(2,1)} %collective-permute-done.16.refs_3_.refs_10_.refs_6_), channel_id=1, source_target_pairs={{0,8},{8,0},{16,24},{24,16},{1,9},{9,1},{17,25},{25,17},{2,10},{10... | collective-permute-start | bytes 4128776 | tf_op jit(solution)/shard_map/ppermute | solution.py:389
  133.6 10.3 %collective-permute-start.17 = (bf16[256,256]{1,0:T(8,128)(2,1)S(1)}, bf16[256,256]{1,0:T(8,128)(2,1)S(1)}, u32[]{:S(2)}, u32[]{:S(2)}) collective-permute-start(bf16[256,256]{1,0:T(8,128)(2,1)S(1)} %add_convert_fusion.3.refs_0_), channel_id=1, source_target_pairs={{0,1},{1,2},{2,3},{3,4},{4,5},{5,6},{6,7},{7,0},{8,9},{9,10},{10,1... | collective-permute-start | bytes 393224 | tf_op jit(solution)/shard_map/ppermute | solution.py:19
  134.0 10.3 %collective-permute-start.18 = (bf16[256,256]{1,0:T(8,128)(2,1)S(1)}, bf16[256,256]{1,0:T(8,128)(2,1)S(1)}, u32[]{:S(2)}, u32[]{:S(2)}) collective-permute-start(bf16[256,256]{1,0:T(8,128)(2,1)S(1)} %add_convert_fusion.3.refs_0_), channel_id=1, source_target_pairs={{0,2},{1,3},{2,4},{3,5},{4,6},{5,7},{6,0},{7,1},{8,10},{9,11},{10,... | collective-permute-start | bytes 393224 | tf_op jit(solution)/shard_map/ppermute | solution.py:19
  136.5 19.4 %collective-permute-start.19 = (bf16[256,256]{1,0:T(8,128)(2,1)S(1)}, bf16[256,256]{1,0:T(8,128)(2,1)S(1)}, u32[]{:S(2)}, u32[]{:S(2)}) collective-permute-start(bf16[256,256]{1,0:T(8,128)(2,1)S(1)} %add_convert_fusion.3.refs_0_), channel_id=1, source_target_pairs={{0,3},{1,4},{2,5},{3,6},{4,7},{5,0},{6,1},{7,2},{8,11},{9,12},{10,... | collective-permute-start | bytes 393224 | tf_op jit(solution)/shard_map/ppermute | solution.py:19
  143.9 12.1 %collective-permute-start.20 = (bf16[256,256]{1,0:T(8,128)(2,1)S(1)}, bf16[256,256]{1,0:T(8,128)(2,1)S(1)}, u32[]{:S(2)}, u32[]{:S(2)}) collective-permute-start(bf16[256,256]{1,0:T(8,128)(2,1)S(1)} %add_convert_fusion.3.refs_0_), channel_id=1, source_target_pairs={{0,4},{1,5},{2,6},{3,7},{4,0},{5,1},{6,2},{7,3},{8,12},{9,13},{10,... | collective-permute-start | bytes 393224 | tf_op jit(solution)/shard_map/ppermute | solution.py:19
  144.3 11.6 %collective-permute-start.21 = (bf16[256,256]{1,0:T(8,128)(2,1)S(1)}, bf16[256,256]{1,0:T(8,128)(2,1)S(1)}, u32[]{:S(2)}, u32[]{:S(2)}) collective-permute-start(bf16[256,256]{1,0:T(8,128)(2,1)S(1)} %add_convert_fusion.3.refs_0_), channel_id=1, source_target_pairs={{0,5},{1,6},{2,7},{3,0},{4,1},{5,2},{6,3},{7,4},{8,13},{9,14},{10,... | collective-permute-start | bytes 393224 | tf_op jit(solution)/shard_map/ppermute | solution.py:19
  147.2 8.7 %collective-permute-start.22 = (bf16[256,256]{1,0:T(8,128)(2,1)S(1)}, bf16[256,256]{1,0:T(8,128)(2,1)S(1)}, u32[]{:S(2)}, u32[]{:S(2)}) collective-permute-start(bf16[256,256]{1,0:T(8,128)(2,1)S(1)} %add_convert_fusion.3.refs_0_), channel_id=1, source_target_pairs={{0,6},{1,7},{2,0},{3,1},{4,2},{5,3},{6,4},{7,5},{8,14},{9,15},{10,... | collective-permute-start | bytes 393224 | tf_op jit(solution)/shard_map/ppermute | solution.py:19
  162.9 17.0 %collective-permute-start.33 = (bf16[2,64,896]{2,1,0:T(8,128)(2,1)}, bf16[2,64,896]{2,1,0:T(8,128)(2,1)}, u32[]{:S(2)}, u32[]{:S(2)}) collective-permute-start(bf16[2,64,896]{2,1,0:T(8,128)(2,1)} %get-tuple-element.133), channel_id=1, source_target_pairs={{0,96},{32,0},{64,32},{96,64},{1,97},{33,1},{65,33},{97,65},{2,98}... | collective-permute-start | bytes 688136 | tf_op jit(solution)/shard_map/ppermute | solution.py:19
  168.2 11.7 %collective-permute-start.32 = (bf16[2,64,896]{2,1,0:T(8,128)(2,1)}, bf16[2,64,896]{2,1,0:T(8,128)(2,1)}, u32[]{:S(2)}, u32[]{:S(2)}) collective-permute-start(bf16[2,64,896]{2,1,0:T(8,128)(2,1)} %get-tuple-element.132), channel_id=1, source_target_pairs={{0,64},{32,96},{64,0},{96,32},{1,65},{33,97},{65,1},{97,33},{2,66}... | collective-permute-start | bytes 688136 | tf_op jit(solution)/shard_map/ppermute | solution.py:19
  168.2 13.8 %collective-permute-start.31 = (bf16[2,64,896]{2,1,0:T(8,128)(2,1)}, bf16[2,64,896]{2,1,0:T(8,128)(2,1)}, u32[]{:S(2)}, u32[]{:S(2)}) collective-permute-start(bf16[2,64,896]{2,1,0:T(8,128)(2,1)} %get-tuple-element.131), channel_id=1, source_target_pairs={{0,32},{32,64},{64,96},{96,0},{1,33},{33,65},{65,97},{97,1},{2,34}... | collective-permute-start | bytes 688136 | tf_op jit(solution)/shard_map/ppermute | solution.py:19
  169.8 13.6 %collective-permute-start.30 = (bf16[64,896]{1,0:T(8,128)(2,1)}, bf16[64,896]{1,0:T(8,128)(2,1)S(1)}, u32[]{:S(2)}, u32[]{:S(2)}) collective-permute-start(bf16[64,896]{1,0:T(8,128)(2,1)} %copy-done.33), channel_id=1, source_target_pairs={{0,96},{32,0},{64,32},{96,64},{1,97},{33,1},{65,33},{97,65},{2,98}... | collective-permute-start | bytes 344072 | tf_op jit(solution)/shard_map/ppermute | solution.py:19
  172.2 11.4 %collective-permute-start.29 = (bf16[64,896]{1,0:T(8,128)(2,1)}, bf16[64,896]{1,0:T(8,128)(2,1)S(1)}, u32[]{:S(2)}, u32[]{:S(2)}) collective-permute-start(bf16[64,896]{1,0:T(8,128)(2,1)} %copy-done.32), channel_id=1, source_target_pairs={{0,64},{32,96},{64,0},{96,32},{1,65},{33,97},{65,1},{97,33},{2,66}... | collective-permute-start | bytes 344072 | tf_op jit(solution)/shard_map/ppermute | solution.py:19
  187.1 11.1 %collective-permute-start.34 = (bf16[3,64,896]{2,1,0:T(8,128)(2,1)S(1)}, bf16[3,64,896]{2,1,0:T(8,128)(2,1)S(1)}, u32[]{:S(2)}, u32[]{:S(2)}) collective-permute-start(bf16[3,64,896]{2,1,0:T(8,128)(2,1)S(1)} %pad_maximum_fusion.1.refs_0_), channel_id=1, source_target_pairs={{0,32},{32,64},{64,96},{96,0},{1,33},{33,65},{65,97},{97,1},{2,34}... | collective-permute-start | bytes 1032200 | tf_op jit(solution)/shard_map/ppermute | solution.py:19
  187.2 14.7 %collective-permute-start.35 = (bf16[3,64,896]{2,1,0:T(8,128)(2,1)S(1)}, bf16[3,64,896]{2,1,0:T(8,128)(2,1)S(1)}, u32[]{:S(2)}, u32[]{:S(2)}) collective-permute-start(bf16[3,64,896]{2,1,0:T(8,128)(2,1)S(1)} %pad_maximum_fusion.1.refs_0_), channel_id=1, source_target_pairs={{0,64},{32,96},{64,0},{96,32},{1,65},{33,97},{65,1},{97,33},{2,66}... | collective-permute-start | bytes 1032200 | tf_op jit(solution)/shard_map/ppermute | solution.py:19
  191.6 10.3 %collective-permute-start.36 = (bf16[3,64,896]{2,1,0:T(8,128)(2,1)S(1)}, bf16[3,64,896]{2,1,0:T(8,128)(2,1)S(1)}, u32[]{:S(2)}, u32[]{:S(2)}) collective-permute-start(bf16[3,64,896]{2,1,0:T(8,128)(2,1)S(1)} %pad_maximum_fusion.1.refs_0_), channel_id=1, source_target_pairs={{0,96},{32,0},{64,32},{96,64},{1,97},{33,1},{65,33},{97,65},{2,98}... | collective-permute-start | bytes 1032200 | tf_op jit(solution)/shard_map/ppermute | solution.py:19
  209.4 17.9 %all-to-all-start.1 = ((bf16[8,256,256]{2,1,0:T(8,128)(2,1)}), bf16[8,256,256]{2,1,0:T(8,128)(2,1)}, u32[]{:S(2)}, u32[]{:S(2)}) async-start(bf16[8,256,256]{2,1,0:T(8,128)(2,1)} %copy-done.13), calls=%async_computation.1 | async-start | bytes 2097152 | tf_op jit(solution)/shard_map/all_to_all | solution.py:331
  215.7 98.7 %reduce-scatter.2.cloned.1.call-start = ((), (), s32[]{:S(2)}) async-start(), calls=%async_computation.4 | async-start | bytes 2359296 | tf_op jit(solution)/shard_map/reduce_scatter | solution.py:462
  229.6 8.9 %collective-permute-start.37 = (bf16[256,256]{1,0:T(8,128)(2,1)S(1)}, bf16[256,256]{1,0:T(8,128)(2,1)S(1)}, u32[]{:S(2)}, u32[]{:S(2)}) collective-permute-start(bf16[256,256]{1,0:T(8,128)(2,1)S(1)} %add_convert_fusion.2.refs_0_), channel_id=1, source_target_pairs={{0,1},{1,2},{2,3},{3,4},{4,5},{5,6},{6,7},{7,0},{8,9},{9,10},{10,1... | collective-permute-start | bytes 393224 | tf_op jit(solution)/shard_map/ppermute | solution.py:19
  230.5 8.8 %collective-permute-start.38 = (bf16[256,256]{1,0:T(8,128)(2,1)S(1)}, bf16[256,256]{1,0:T(8,128)(2,1)S(1)}, u32[]{:S(2)}, u32[]{:S(2)}) collective-permute-start(bf16[256,256]{1,0:T(8,128)(2,1)S(1)} %add_convert_fusion.2.refs_0_), channel_id=1, source_target_pairs={{0,2},{1,3},{2,4},{3,5},{4,6},{5,7},{6,0},{7,1},{8,10},{9,11},{10,... | collective-permute-start | bytes 393224 | tf_op jit(solution)/shard_map/ppermute | solution.py:19
  233.1 12.2 %collective-permute-start.39 = (bf16[256,256]{1,0:T(8,128)(2,1)S(1)}, bf16[256,256]{1,0:T(8,128)(2,1)S(1)}, u32[]{:S(2)}, u32[]{:S(2)}) collective-permute-start(bf16[256,256]{1,0:T(8,128)(2,1)S(1)} %add_convert_fusion.2.refs_0_), channel_id=1, source_target_pairs={{0,3},{1,4},{2,5},{3,6},{4,7},{5,0},{6,1},{7,2},{8,11},{9,12},{10,... | collective-permute-start | bytes 393224 | tf_op jit(solution)/shard_map/ppermute | solution.py:19
  235.1 10.2 %collective-permute-start.40 = (bf16[256,256]{1,0:T(8,128)(2,1)S(1)}, bf16[256,256]{1,0:T(8,128)(2,1)S(1)}, u32[]{:S(2)}, u32[]{:S(2)}) collective-permute-start(bf16[256,256]{1,0:T(8,128)(2,1)S(1)} %add_convert_fusion.2.refs_0_), channel_id=1, source_target_pairs={{0,4},{1,5},{2,6},{3,7},{4,0},{5,1},{6,2},{7,3},{8,12},{9,13},{10,... | collective-permute-start | bytes 393224 | tf_op jit(solution)/shard_map/ppermute | solution.py:19
  235.7 9.7 %collective-permute-start.41 = (bf16[256,256]{1,0:T(8,128)(2,1)S(1)}, bf16[256,256]{1,0:T(8,128)(2,1)S(1)}, u32[]{:S(2)}, u32[]{:S(2)}) collective-permute-start(bf16[256,256]{1,0:T(8,128)(2,1)S(1)} %add_convert_fusion.2.refs_0_), channel_id=1, source_target_pairs={{0,5},{1,6},{2,7},{3,0},{4,1},{5,2},{6,3},{7,4},{8,13},{9,14},{10,... | collective-permute-start | bytes 393224 | tf_op jit(solution)/shard_map/ppermute | solution.py:19
  250.1 9.6 %collective-permute-start.44 = (bf16[64,1792]{1,0:T(8,128)(2,1)S(1)}, bf16[64,1792]{1,0:T(8,128)(2,1)S(1)}, u32[]{:S(2)}, u32[]{:S(2)}) collective-permute-start(bf16[64,1792]{1,0:T(8,128)(2,1)S(1)} %get-tuple-element.150), channel_id=1, source_target_pairs={{0,32},{32,64},{64,96},{96,0},{1,33},{33,65},{65,97},{97,1},{2,34}... | collective-permute-start | bytes 688136 | tf_op jit(solution)/shard_map/ppermute | solution.py:19
  251.3 10.9 %collective-permute-start.45 = (bf16[64,1792]{1,0:T(8,128)(2,1)S(1)}, bf16[64,1792]{1,0:T(8,128)(2,1)S(1)}, u32[]{:S(2)}, u32[]{:S(2)}) collective-permute-start(bf16[64,1792]{1,0:T(8,128)(2,1)S(1)} %get-tuple-element.151), channel_id=1, source_target_pairs={{0,64},{32,96},{64,0},{96,32},{1,65},{33,97},{65,1},{97,33},{2,66}... | collective-permute-start | bytes 688136 | tf_op jit(solution)/shard_map/ppermute | solution.py:19
  262.6 14.5 %collective-permute-start.47 = (bf16[2,64,1792]{2,1,0:T(8,128)(2,1)S(1)}, bf16[2,64,1792]{2,1,0:T(8,128)(2,1)S(1)}, u32[]{:S(2)}, u32[]{:S(2)}) collective-permute-start(bf16[2,64,1792]{2,1,0:T(8,128)(2,1)S(1)} %pad_maximum_fusion.refs_0_), channel_id=1, source_target_pairs={{0,32},{32,64},{64,96},{96,0},{1,33},{33,65},{65,97},{97,1},{2,34}... | collective-permute-start | bytes 1376264 | tf_op jit(solution)/shard_map/ppermute | solution.py:19
  262.7 19.3 %collective-permute-start.48 = (bf16[2,64,1792]{2,1,0:T(8,128)(2,1)S(1)}, bf16[2,64,1792]{2,1,0:T(8,128)(2,1)S(1)}, u32[]{:S(2)}, u32[]{:S(2)}) collective-permute-start(bf16[2,64,1792]{2,1,0:T(8,128)(2,1)S(1)} %pad_maximum_fusion.refs_0_), channel_id=1, source_target_pairs={{0,64},{32,96},{64,0},{96,32},{1,65},{33,97},{65,1},{97,33},{2,66}... | collective-permute-start | bytes 1376264 | tf_op jit(solution)/shard_map/ppermute | solution.py:19
  266.3 15.7 %collective-permute-start.49 = (bf16[2,64,1792]{2,1,0:T(8,128)(2,1)S(1)}, bf16[2,64,1792]{2,1,0:T(8,128)(2,1)S(1)}, u32[]{:S(2)}, u32[]{:S(2)}) collective-permute-start(bf16[2,64,1792]{2,1,0:T(8,128)(2,1)S(1)} %pad_maximum_fusion.refs_0_), channel_id=1, source_target_pairs={{0,96},{32,0},{64,32},{96,64},{1,97},{33,1},{65,33},{97,65},{2,98}... | collective-permute-start | bytes 1376264 | tf_op jit(solution)/shard_map/ppermute | solution.py:19
  (42 other events, 250.8 us)
Sparse Core Ops, SparseCore 0:
  54.7 64.7 all-gather.2
  250.2 43.3 reduce-scatter.1

commit v2 on v1

--- a/solution.py
+++ b/solution.py
@@ -459,7 +459,7 @@
     own, parts = hidden_grad_wide(idx, grad_chunks, down_2)
 
     received = send(parts, "section", 4)
-    out_sum = lax.psum_scatter(after(out_part, own), "tensor", scatter_dimension=0, tiled=True)
+    out_sum = lax.psum_scatter(after(out_part, middle_grad), "tensor", scatter_dimension=0, tiled=True)
     outputs = (mid_rows.astype(F32) + out_sum).astype(BF)
 
     gate_2, = into_vmem(after(gate_wide, own))

time: 324 us -> 330 us (1.019)
  waiting for transfers between devices: 88.9 us -> 101 us
  blocking collectives: 27.1 us -> 22.6 us
    ppermute x42, waiting for transfers between devices: 52.2 us -> 63.8 us  [send(): lax.ppermute(p, axis, ring(n, r))]
    all_to_all x1, blocking collectives: 27.1 us -> 22.6 us  [add_over_tensor(): lax.all_to_all(parts, 'tensor', split_axis=0, concat_axis=0, tiled=True)]
    unnamed x72 -> x76, local copies, waits for them, and re-layouts: 34.6 us -> 32.6 us
  transfers between devices with their start and end apart: 54 -> 54, of which waited for: 22 -> 25; matrix products, arithmetic and copies ran while one was open for 2% -> 2% of each run, Pallas kernels for 9% -> 9%
where the time goes in v2:
time: 330 us; the launch traced here: 329 us
  starting transfers between devices  105 us (32%)
  waiting for transfers between devices  101 us (31%)
  Pallas kernels  41.3 us (13%)
  local copies, waits for them, and re-layouts  32.6 us (10%)
  blocking collectives  22.6 us (7%)
  between operations  15.9 us (5%)
  other arithmetic  10 us (3%)
    ppermute x42, starting transfers between devices, send(): lax.ppermute(p, axis, ring(n, r))  70.2 us
    ppermute x42, waiting for transfers between devices, send(): lax.ppermute(p, axis, ring(n, r))  63.8 us
    pallas_call x9, Pallas kernels, call(): pl.pallas_call(kernel, in_specs=[SM] + [VM] * len(operands), out_specs=[V...  38.3 us
    unnamed x76, local copies, waits for them, and re-layouts  32.6 us
    ppermute x4, waiting for transfers between devices, hand_out(): return lax.ppermute(piece, ('dp', 'tensor'), perm)  24.4 us
    all_to_all x1, blocking collectives, add_over_tensor(): lax.all_to_all(parts, 'tensor', split_axis=0, concat_axis=0, tiled=True)  22.6 us
    all_to_all x2, starting transfers between devices, add_over_tensor(): lax.all_to_all(parts, 'tensor', split_axis=0, concat_axis=0, tiled=True)  19.9 us
    ppermute x4, starting transfers between devices, hand_out(): return lax.ppermute(piece, ('dp', 'tensor'), perm)  13.8 us
  transfers between devices with their start and end apart: 54, of which 25 were waited for; matrix products, arithmetic and copies ran while one was open for 2% of the time, Pallas kernels for 9%

profile of v2, /device:TPU:0, one launch (start us, length us, event | category | flops | bytes accessed | tf_op | source)
XLA Modules:
  0.0 328.8 jit_solution(4431276271670892440)
XLA Ops:
  8.9 2.9 collective-permute-start.1
  16.6 3.2 collective-permute-start.5
  23.4 2.4 shard_map.113
  28.9 5.6 %collective-permute-start.11 = (bf16[3,256,896]{2,1,0:T(8,128)(2,1)}, bf16[3,256,896]{2,1,0:T(8,128)(2,1)S(1)}, u32[]{:S(2)}, u32[]{:S(2)}) collective-permute-start(bf16[3,256,896]{2,1,0:T(8,128)(2,1)} %get-tuple-element.108), channel_id=1, source_target_pairs={{0,17},{1,25},{2,16},{3,24},{4,1},{5,9},{6,0},{7,8},{8,21},{9,29},... | collective-permute-start | bytes 4128776 | tf_op jit(solution)/shard_map/ppermute | solution.py:385
  34.5 3.1 copy-done.2
  37.6 3.1 copy-done.4
  41.7 6.7 %shard_map.115 = (f32[2,64,1792]{2,1,0:T(8,128)S(1)}, bf16[2,64,1792]{2,1,0:T(8,128)(2,1)}, bf16[2,64,1792]{2,1,0:T(8,128)(2,1)}, bf16[2,64,1792]{2,1,0:T(8,128)(2,1)}, bf16[32,2048]{1,0:T(8,128)(2,1)}) custom-call(s32[3]{0:T(128)S(1)} %pad_add_fusion.idx_ref, bf16[256,256]{1,0:T(8,128)(2,1)S(1)} %bitcast.91, ...), custom_call_target="tpu_custom_call" | custom-call | flops 3758096384 | bytes 14680064 | tf_op jit(solution)/shard_map/pallas_call | solution.py:63
  49.3 4.0 %collective-permute-start.9 = (bf16[2,64,1792]{2,1,0:T(8,128)(2,1)}, bf16[2,64,1792]{2,1,0:T(8,128)(2,1)S(1)}, u32[]{:S(2)}, u32[]{:S(2)}) collective-permute-start(bf16[2,64,1792]{2,1,0:T(8,128)(2,1)} %get-tuple-element.99), channel_id=1, source_target_pairs={{0,96},{32,0},{64,32},{96,64},{1,97},{33,1},{65,33},{97,65},{2,98}... | collective-permute-start | bytes 1376264 | tf_op jit(solution)/shard_map/ppermute | solution.py:19
  55.3 13.4 %collective-permute-done.11.refs_4_.refs_11_.refs_7_ = bf16[3,256,896]{2,1,0:T(8,128)(2,1)S(1)} collective-permute-done((bf16[3,256,896]{2,1,0:T(8,128)(2,1)}, bf16[3,256,896]{2,1,0:T(8,128)(2,1)S(1)}, u32[]{:S(2)}, u32[]{:S(2)}) %collective-permute-start.11) | collective-permute-done | bytes 1376288 | tf_op jit(solution)/shard_map/ppermute | solution.py:385
  68.7 6.2 %collective-permute-start.16 = (bf16[3,256,896]{2,1,0:T(8,128)(2,1)}, bf16[3,256,896]{2,1,0:T(8,128)(2,1)}, u32[]{:S(2)}, u32[]{:S(2)}) collective-permute-start(bf16[3,256,896]{2,1,0:T(8,128)(2,1)} %get-tuple-element.109), channel_id=1, source_target_pairs={{0,16},{1,24},{2,17},{3,25},{4,0},{5,8},{6,1},{7,9},{8,20},{9,28},... | collective-permute-start | bytes 4128776 | tf_op jit(solution)/shard_map/ppermute | solution.py:385
  78.8 3.9 %collective-permute-start.13 = (bf16[64,1792]{1,0:T(8,128)(2,1)S(1)}, bf16[64,1792]{1,0:T(8,128)(2,1)S(1)}, u32[]{:S(2)}, u32[]{:S(2)}) collective-permute-start(bf16[64,1792]{1,0:T(8,128)(2,1)S(1)} %multiply_convert_fusion.2.refs_0_), channel_id=1, source_target_pairs={{0,64},{32,96},{64,0},{96,32},{1,65},{33,97},{65,1},{97,33},{2,66}... | collective-permute-start | bytes 688136 | tf_op jit(solution)/shard_map/ppermute | solution.py:19
  83.6 3.1 copy-done
  87.2 4.2 %collective-permute-done.12.refs_1_ = bf16[64,1792]{1,0:T(8,128)(2,1)S(1)} collective-permute-done((bf16[64,1792]{1,0:T(8,128)(2,1)S(1)}, bf16[64,1792]{1,0:T(8,128)(2,1)S(1)}, u32[]{:S(2)}, u32[]{:S(2)}) %collective-permute-start.12) | collective-permute-done | bytes 229408 | tf_op jit(solution)/shard_map/ppermute | solution.py:19
  92.1 2.6 shard_map.117
  95.7 11.0 %collective-permute-done.15.refs_2_.refs_9_.refs_5_ = bf16[3,256,896]{2,1,0:T(8,128)(2,1)} collective-permute-done((bf16[3,256,896]{2,1,0:T(8,128)(2,1)}, bf16[3,256,896]{2,1,0:T(8,128)(2,1)}, u32[]{:S(2)}, u32[]{:S(2)}) %collective-permute-start.15) | collective-permute-done | bytes 1376288 | tf_op jit(solution)/shard_map/ppermute | solution.py:385
  106.7 13.2 %all-to-all-start = ((bf16[8,256,256]{2,1,0:T(8,128)(2,1)}), bf16[8,256,256]{2,1,0:T(8,128)(2,1)}, u32[]{:S(2)}, u32[]{:S(2)}) async-start(bf16[8,256,256]{2,1,0:T(8,128)(2,1)} %copy-done.12), calls=%async_computation | async-start | bytes 2097152 | tf_op jit(solution)/shard_map/all_to_all | solution.py:331
  120.4 11.4 %all-to-all-done = bf16[8,256,256]{2,1,0:T(8,128)(2,1)} async-done(((bf16[8,256,256]{2,1,0:T(8,128)(2,1)}), bf16[8,256,256]{2,1,0:T(8,128)(2,1)}, u32[]{:S(2)}, u32[]{:S(2)}) %all-to-all-start) | async-done | bytes 1048608 | tf_op jit(solution)/shard_map/all_to_all | solution.py:331
  134.5 2.5 collective-permute-start.18
  138.1 5.8 %collective-permute-done.17.refs_1_ = bf16[256,256]{1,0:T(8,128)(2,1)S(1)} collective-permute-done((bf16[256,256]{1,0:T(8,128)(2,1)S(1)}, bf16[256,256]{1,0:T(8,128)(2,1)S(1)}, u32[]{:S(2)}, u32[]{:S(2)}) %collective-permute-start.17) | collective-permute-done | bytes 131104 | tf_op jit(solution)/shard_map/ppermute | solution.py:19
  144.8 2.8 collective-permute-start.21
  151.5 4.0 %shard_map.118 = (f32[64,896]{1,0:T(8,128)S(1)}, bf16[64,896]{1,0:T(8,128)(2,1)S(1)}, bf16[64,896]{1,0:T(8,128)(2,1)S(1)}, bf16[64,896]{1,0:T(8,128)(2,1)S(1)}, bf16[256,256]{1,0:T(8,128)(2,1)S(1)}) custom-call(s32[3]{0:T(128)S(1)} %pad_add_fusion.idx_ref, bf16[256,2048]{1,0:T(8,128)(2,1)S(1)} %bitcast.83, ...), custom_call_target="tpu_custom_call" | custom-call | flops 939524096 | bytes 3670016 | tf_op jit(solution)/shard_map/pallas_call | solution.py:63
  156.3 6.3 %shard_map.119 = (f32[2,64,896]{2,1,0:T(8,128)S(1)}, bf16[2,64,896]{2,1,0:T(8,128)(2,1)}, bf16[2,64,896]{2,1,0:T(8,128)(2,1)}, bf16[2,64,896]{2,1,0:T(8,128)(2,1)}, bf16[32,2048]{1,0:T(8,128)(2,1)S(1)}) custom-call(s32[3]{0:T(128)S(1)} %pad_add_fusion.idx_ref, bf16[256,256]{1,0:T(8,128)(2,1)S(1)} %add_convert_fusion.3.refs_0_, ...), custom_call_target="tpu_custom_call" | custom-call | flops 1879048192 | bytes 7340032 | tf_op jit(solution)/shard_map/pallas_call | solution.py:63
  163.2 5.0 %collective-permute-start.33 = (bf16[2,64,896]{2,1,0:T(8,128)(2,1)}, bf16[2,64,896]{2,1,0:T(8,128)(2,1)}, u32[]{:S(2)}, u32[]{:S(2)}) collective-permute-start(bf16[2,64,896]{2,1,0:T(8,128)(2,1)} %get-tuple-element.133), channel_id=1, source_target_pairs={{0,96},{32,0},{64,32},{96,64},{1,97},{33,1},{65,33},{97,65},{2,98}... | collective-permute-start | bytes 688136 | tf_op jit(solution)/shard_map/ppermute | solution.py:19
  169.7 2.4 collective-permute-start.30
  172.2 2.3 collective-permute-start.29
  174.5 5.4 %collective-permute-done.33 = bf16[2,64,896]{2,1,0:T(8,128)(2,1)} collective-permute-done((bf16[2,64,896]{2,1,0:T(8,128)(2,1)}, bf16[2,64,896]{2,1,0:T(8,128)(2,1)}, u32[]{:S(2)}, u32[]{:S(2)}) %collective-permute-start.33) | collective-permute-done | bytes 229408 | tf_op jit(solution)/shard_map/ppermute | solution.py:19
  183.6 3.5 %collective-permute-done.28 = bf16[64,896]{1,0:T(8,128)(2,1)S(1)} collective-permute-done((bf16[64,896]{1,0:T(8,128)(2,1)}, bf16[64,896]{1,0:T(8,128)(2,1)S(1)}, u32[]{:S(2)}, u32[]{:S(2)}) %collective-permute-start.28) | collective-permute-done | bytes 114720 | tf_op jit(solution)/shard_map/ppermute | solution.py:19
  187.3 4.3 %collective-permute-start.35 = (bf16[3,64,896]{2,1,0:T(8,128)(2,1)S(1)}, bf16[3,64,896]{2,1,0:T(8,128)(2,1)S(1)}, u32[]{:S(2)}, u32[]{:S(2)}) collective-permute-start(bf16[3,64,896]{2,1,0:T(8,128)(2,1)S(1)} %pad_maximum_fusion.1.refs_0_), channel_id=1, source_target_pairs={{0,64},{32,96},{64,0},{96,32},{1,65},{33,97},{65,1},{97,33},{2,66}... | collective-permute-start | bytes 1032200 | tf_op jit(solution)/shard_map/ppermute | solution.py:19
  191.9 5.9 %collective-permute-done.34.refs_1_ = bf16[3,64,896]{2,1,0:T(8,128)(2,1)S(1)} collective-permute-done((bf16[3,64,896]{2,1,0:T(8,128)(2,1)S(1)}, bf16[3,64,896]{2,1,0:T(8,128)(2,1)S(1)}, u32[]{:S(2)}, u32[]{:S(2)}) %collective-permute-start.34) | collective-permute-done | bytes 344096 | tf_op jit(solution)/shard_map/ppermute | solution.py:19
  197.8 3.7 %collective-permute-done.35.refs_2_ = bf16[3,64,896]{2,1,0:T(8,128)(2,1)S(1)} collective-permute-done((bf16[3,64,896]{2,1,0:T(8,128)(2,1)S(1)}, bf16[3,64,896]{2,1,0:T(8,128)(2,1)S(1)}, u32[]{:S(2)}, u32[]{:S(2)}) %collective-permute-start.35) | collective-permute-done | bytes 344096 | tf_op jit(solution)/shard_map/ppermute | solution.py:19
  201.6 5.0 %shard_map.120 = bf16[8,256,256]{2,1,0:T(8,128)(2,1)S(1)} custom-call(s32[3]{0:T(128)S(1)} %pad_add_fusion.idx_ref, bf16[3,64,896]{2,1,0:T(8,128)(2,1)S(1)} %pad_maximum_fusion.1.refs_0_, bf16[3,64,896]{2,1,0:T(8,128)(2,1)S(1)} %collective-permute-done.34.refs_1_, bf16[3,64,896]{2,1,0:T(8,128)(2,1)S(1)} %collective-permute-done.35.refs_2_, ...), custom_call_target="tpu_custom_call" | custom-call | flops 1879048192 | bytes 7340032 | tf_op jit(solution)/shard_map/pallas_call | solution.py:63
  209.1 6.7 %all-to-all-start.1 = ((bf16[8,256,256]{2,1,0:T(8,128)(2,1)}), bf16[8,256,256]{2,1,0:T(8,128)(2,1)}, u32[]{:S(2)}, u32[]{:S(2)}) async-start(bf16[8,256,256]{2,1,0:T(8,128)(2,1)} %copy-done.13), calls=%async_computation.1 | async-start | bytes 2097152 | tf_op jit(solution)/shard_map/all_to_all | solution.py:331
  220.4 3.9 %shard_map.121 = f32[256,2048]{1,0:T(8,128)S(1)} custom-call(s32[3]{0:T(128)S(1)} %pad_add_fusion.idx_ref, bf16[3,64,896]{2,1,0:T(8,128)(2,1)S(1)} %pad_maximum_fusion.1.refs_0_, bf16[3,64,896]{2,1,0:T(8,128)(2,1)S(1)} %collective-permute-done.34.refs_1_, bf16[3,64,896]{2,1,0:T(8,128)(2,1)S(1)} %copy-done.15, bf16[3,64,896]{2,1,0:T(8,128)(2,1)S(1)} %copy-done.17, ...), custom_call_target="tpu_custom_call" | custom-call | flops 939524096 | bytes 3670016 | tf_op jit(solution)/shard_map/pallas_call | solution.py:63
  230.6 2.6 collective-permute-start.38
  239.5 2.4 collective-permute-start.43
  241.8 3.1 copy-done.1
  247.4 4.3 %collective-permute-done.42.refs_6_ = bf16[256,256]{1,0:T(8,128)(2,1)S(1)} collective-permute-done((bf16[256,256]{1,0:T(8,128)(2,1)S(1)}, bf16[256,256]{1,0:T(8,128)(2,1)S(1)}, u32[]{:S(2)}, u32[]{:S(2)}) %collective-permute-start.42) | collective-permute-done | bytes 131104 | tf_op jit(solution)/shard_map/ppermute | solution.py:19
  251.7 3.8 %collective-permute-done.43.refs_7_ = bf16[256,256]{1,0:T(8,128)(2,1)S(1)} collective-permute-done((bf16[256,256]{1,0:T(8,128)(2,1)S(1)}, bf16[256,256]{1,0:T(8,128)(2,1)S(1)}, u32[]{:S(2)}, u32[]{:S(2)}) %collective-permute-start.43) | collective-permute-done | bytes 131104 | tf_op jit(solution)/shard_map/ppermute | solution.py:19
  255.5 2.9 shard_map.123
  259.0 4.9 %collective-permute-start.45 = (bf16[64,1792]{1,0:T(8,128)(2,1)S(1)}, bf16[64,1792]{1,0:T(8,128)(2,1)S(1)}, u32[]{:S(2)}, u32[]{:S(2)}) collective-permute-start(bf16[64,1792]{1,0:T(8,128)(2,1)S(1)} %get-tuple-element.151), channel_id=1, source_target_pairs={{0,64},{32,96},{64,0},{96,32},{1,65},{33,97},{65,1},{97,33},{2,66}... | collective-permute-start | bytes 688136 | tf_op jit(solution)/shard_map/ppermute | solution.py:19
  263.9 3.2 copy-done.3
  267.5 5.2 %collective-permute-done.45 = bf16[64,1792]{1,0:T(8,128)(2,1)S(1)} collective-permute-done((bf16[64,1792]{1,0:T(8,128)(2,1)S(1)}, bf16[64,1792]{1,0:T(8,128)(2,1)S(1)}, u32[]{:S(2)}, u32[]{:S(2)}) %collective-permute-start.45) | collective-permute-done | bytes 229408 | tf_op jit(solution)/shard_map/ppermute | solution.py:19
  272.7 2.6 collective-permute-done.46
  275.8 5.1 %collective-permute-start.48 = (bf16[2,64,1792]{2,1,0:T(8,128)(2,1)S(1)}, bf16[2,64,1792]{2,1,0:T(8,128)(2,1)S(1)}, u32[]{:S(2)}, u32[]{:S(2)}) collective-permute-start(bf16[2,64,1792]{2,1,0:T(8,128)(2,1)S(1)} %pad_maximum_fusion.refs_0_), channel_id=1, source_target_pairs={{0,64},{32,96},{64,0},{96,32},{1,65},{33,97},{65,1},{97,33},{2,66}... | collective-permute-start | bytes 1376264 | tf_op jit(solution)/shard_map/ppermute | solution.py:19
  281.5 4.5 %collective-permute-done.47.refs_1_ = bf16[2,64,1792]{2,1,0:T(8,128)(2,1)S(1)} collective-permute-done((bf16[2,64,1792]{2,1,0:T(8,128)(2,1)S(1)}, bf16[2,64,1792]{2,1,0:T(8,128)(2,1)S(1)}, u32[]{:S(2)}, u32[]{:S(2)}) %collective-permute-start.47) | collective-permute-done | bytes 458784 | tf_op jit(solution)/shard_map/ppermute | solution.py:19
  286.0 6.4 %collective-permute-done.48.refs_2_ = bf16[2,64,1792]{2,1,0:T(8,128)(2,1)S(1)} collective-permute-done((bf16[2,64,1792]{2,1,0:T(8,128)(2,1)S(1)}, bf16[2,64,1792]{2,1,0:T(8,128)(2,1)S(1)}, u32[]{:S(2)}, u32[]{:S(2)}) %collective-permute-start.48) | collective-permute-done | bytes 458784 | tf_op jit(solution)/shard_map/ppermute | solution.py:19
  292.4 4.5 %shard_map.126 = bf16[8,256,256]{2,1,0:T(8,128)(2,1)S(1)} custom-call(s32[3]{0:T(128)S(1)} %pad_add_fusion.idx_ref, bf16[2,64,1792]{2,1,0:T(8,128)(2,1)S(1)} %pad_maximum_fusion.refs_0_, bf16[2,64,1792]{2,1,0:T(8,128)(2,1)S(1)} %collective-permute-done.47.refs_1_, bf16[2,64,1792]{2,1,0:T(8,128)(2,1)S(1)} %collective-permute-done.48.refs_2_, ...), custom_call_target="tpu_custom_call" | custom-call | flops 3758096384 | bytes 14680064 | tf_op jit(solution)/shard_map/pallas_call | solution.py:63
  296.9 22.6 %all_to_all.15 = bf16[8,256,256]{2,1,0:T(8,128)(2,1)S(1)} all-to-all(bf16[8,256,256]{2,1,0:T(8,128)(2,1)S(1)} %shard_map.126), channel_id=1, replica_groups=mesh['section'=4,'dp'=4,'tensor'=8] {'tensor'}, dimensions={0} | all-to-all | bytes 2097152 | tf_op jit(solution)/shard_map/all_to_all | solution.py:331
  (173 shorter events, 65.5 us)
Async XLA Ops:
  7.2 126.1 %all-gather.3.cloned.1.call-start = ((), (), s32[]{:S(2)}) async-start(), calls=%async_computation.5 | async-start | bytes 1179648 | tf_op jit(solution)/shard_map/all_gather | solution.py:423
  7.2 9.4 %collective-permute-start = (bf16[256,256]{1,0:T(8,128)(2,1)}, bf16[256,256]{1,0:T(8,128)(2,1)S(1)}, u32[]{:S(2)}, u32[]{:S(2)}) collective-permute-start(bf16[256,256]{1,0:T(8,128)(2,1)} %bitcast.84), channel_id=1, source_target_pairs={{0,1},{1,2},{2,3},{3,4},{4,5},{5,6},{6,7},{7,0},{8,9},{9,10},{10,1... | collective-permute-start | bytes 393224 | tf_op jit(solution)/shard_map/ppermute | solution.py:19
  8.9 10.8 %collective-permute-start.1 = (bf16[256,256]{1,0:T(8,128)(2,1)}, bf16[256,256]{1,0:T(8,128)(2,1)S(1)}, u32[]{:S(2)}, u32[]{:S(2)}) collective-permute-start(bf16[256,256]{1,0:T(8,128)(2,1)} %bitcast.85), channel_id=1, source_target_pairs={{0,2},{1,3},{2,4},{3,5},{4,6},{5,7},{6,0},{7,1},{8,10},{9,11},{10,... | collective-permute-start | bytes 393224 | tf_op jit(solution)/shard_map/ppermute | solution.py:19
  11.8 13.9 %collective-permute-start.2 = (bf16[256,256]{1,0:T(8,128)(2,1)}, bf16[256,256]{1,0:T(8,128)(2,1)S(1)}, u32[]{:S(2)}, u32[]{:S(2)}) collective-permute-start(bf16[256,256]{1,0:T(8,128)(2,1)} %bitcast.86), channel_id=1, source_target_pairs={{0,3},{1,4},{2,5},{3,6},{4,7},{5,0},{6,1},{7,2},{8,11},{9,12},{10,... | collective-permute-start | bytes 393224 | tf_op jit(solution)/shard_map/ppermute | solution.py:19
  14.1 11.6 %collective-permute-start.3 = (bf16[256,256]{1,0:T(8,128)(2,1)}, bf16[256,256]{1,0:T(8,128)(2,1)S(1)}, u32[]{:S(2)}, u32[]{:S(2)}) collective-permute-start(bf16[256,256]{1,0:T(8,128)(2,1)} %bitcast.87), channel_id=1, source_target_pairs={{0,4},{1,5},{2,6},{3,7},{4,0},{5,1},{6,2},{7,3},{8,12},{9,13},{10,... | collective-permute-start | bytes 393224 | tf_op jit(solution)/shard_map/ppermute | solution.py:19
  14.7 11.1 %collective-permute-start.4 = (bf16[256,256]{1,0:T(8,128)(2,1)}, bf16[256,256]{1,0:T(8,128)(2,1)S(1)}, u32[]{:S(2)}, u32[]{:S(2)}) collective-permute-start(bf16[256,256]{1,0:T(8,128)(2,1)} %bitcast.88), channel_id=1, source_target_pairs={{0,5},{1,6},{2,7},{3,0},{4,1},{5,2},{6,3},{7,4},{8,13},{9,14},{10,... | collective-permute-start | bytes 393224 | tf_op jit(solution)/shard_map/ppermute | solution.py:19
  16.6 9.2 %collective-permute-start.5 = (bf16[256,256]{1,0:T(8,128)(2,1)}, bf16[256,256]{1,0:T(8,128)(2,1)S(1)}, u32[]{:S(2)}, u32[]{:S(2)}) collective-permute-start(bf16[256,256]{1,0:T(8,128)(2,1)} %bitcast.89), channel_id=1, source_target_pairs={{0,6},{1,7},{2,0},{3,1},{4,2},{5,3},{6,4},{7,5},{8,14},{9,15},{10,... | collective-permute-start | bytes 393224 | tf_op jit(solution)/shard_map/ppermute | solution.py:19
  26.9 28.4 %collective-permute-start.10 = (bf16[3,256,896]{2,1,0:T(8,128)(2,1)}, bf16[3,256,896]{2,1,0:T(8,128)(2,1)S(1)}, u32[]{:S(2)}, u32[]{:S(2)}) collective-permute-start(bf16[3,256,896]{2,1,0:T(8,128)(2,1)} %get-tuple-element.109), channel_id=1, source_target_pairs={{0,0},{1,8},{2,1},{3,9},{4,16},{5,24},{6,17},{7,25},{8,4},{9,12},{... | collective-permute-start | bytes 4128776 | tf_op jit(solution)/shard_map/ppermute | solution.py:385
  28.9 39.8 %collective-permute-start.11 = (bf16[3,256,896]{2,1,0:T(8,128)(2,1)}, bf16[3,256,896]{2,1,0:T(8,128)(2,1)S(1)}, u32[]{:S(2)}, u32[]{:S(2)}) collective-permute-start(bf16[3,256,896]{2,1,0:T(8,128)(2,1)} %get-tuple-element.108), channel_id=1, source_target_pairs={{0,17},{1,25},{2,16},{3,24},{4,1},{5,9},{6,0},{7,8},{8,21},{9,29},... | collective-permute-start | bytes 4128776 | tf_op jit(solution)/shard_map/ppermute | solution.py:385
  49.3 25.6 %collective-permute-start.9 = (bf16[2,64,1792]{2,1,0:T(8,128)(2,1)}, bf16[2,64,1792]{2,1,0:T(8,128)(2,1)S(1)}, u32[]{:S(2)}, u32[]{:S(2)}) collective-permute-start(bf16[2,64,1792]{2,1,0:T(8,128)(2,1)} %get-tuple-element.99), channel_id=1, source_target_pairs={{0,96},{32,0},{64,32},{96,64},{1,97},{33,1},{65,33},{97,65},{2,98}... | collective-permute-start | bytes 1376264 | tf_op jit(solution)/shard_map/ppermute | solution.py:19
  53.3 21.6 %collective-permute-start.8 = (bf16[2,64,1792]{2,1,0:T(8,128)(2,1)}, bf16[2,64,1792]{2,1,0:T(8,128)(2,1)}, u32[]{:S(2)}, u32[]{:S(2)}) collective-permute-start(bf16[2,64,1792]{2,1,0:T(8,128)(2,1)} %get-tuple-element.98), channel_id=1, source_target_pairs={{0,64},{32,96},{64,0},{96,32},{1,65},{33,97},{65,1},{97,33},{2,66}... | collective-permute-start | bytes 1376264 | tf_op jit(solution)/shard_map/ppermute | solution.py:19
  53.3 23.0 %collective-permute-start.7 = (bf16[2,64,1792]{2,1,0:T(8,128)(2,1)}, bf16[2,64,1792]{2,1,0:T(8,128)(2,1)}, u32[]{:S(2)}, u32[]{:S(2)}) collective-permute-start(bf16[2,64,1792]{2,1,0:T(8,128)(2,1)} %get-tuple-element.97), channel_id=1, source_target_pairs={{0,32},{32,64},{64,96},{96,0},{1,33},{33,65},{65,97},{97,1},{2,34}... | collective-permute-start | bytes 1376264 | tf_op jit(solution)/shard_map/ppermute | solution.py:19
  68.7 38.0 %collective-permute-start.15 = (bf16[3,256,896]{2,1,0:T(8,128)(2,1)}, bf16[3,256,896]{2,1,0:T(8,128)(2,1)}, u32[]{:S(2)}, u32[]{:S(2)}) collective-permute-start(bf16[3,256,896]{2,1,0:T(8,128)(2,1)} %get-tuple-element.108), channel_id=1, source_target_pairs={{0,1},{1,9},{2,0},{3,8},{4,17},{5,25},{6,16},{7,24},{8,5},{9,13},{... | collective-permute-start | bytes 4128776 | tf_op jit(solution)/shard_map/ppermute | solution.py:385
  68.7 38.0 %collective-permute-start.16 = (bf16[3,256,896]{2,1,0:T(8,128)(2,1)}, bf16[3,256,896]{2,1,0:T(8,128)(2,1)}, u32[]{:S(2)}, u32[]{:S(2)}) collective-permute-start(bf16[3,256,896]{2,1,0:T(8,128)(2,1)} %get-tuple-element.109), channel_id=1, source_target_pairs={{0,16},{1,24},{2,17},{3,25},{4,0},{5,8},{6,1},{7,9},{8,20},{9,28},... | collective-permute-start | bytes 4128776 | tf_op jit(solution)/shard_map/ppermute | solution.py:385
  78.1 13.4 %collective-permute-start.12 = (bf16[64,1792]{1,0:T(8,128)(2,1)S(1)}, bf16[64,1792]{1,0:T(8,128)(2,1)S(1)}, u32[]{:S(2)}, u32[]{:S(2)}) collective-permute-start(bf16[64,1792]{1,0:T(8,128)(2,1)S(1)} %multiply_convert_fusion.2.refs_0_), channel_id=1, source_target_pairs={{0,32},{32,64},{64,96},{96,0},{1,33},{33,65},{65,97},{97,1},{2,34}... | collective-permute-start | bytes 688136 | tf_op jit(solution)/shard_map/ppermute | solution.py:19
  78.8 12.6 %collective-permute-start.13 = (bf16[64,1792]{1,0:T(8,128)(2,1)S(1)}, bf16[64,1792]{1,0:T(8,128)(2,1)S(1)}, u32[]{:S(2)}, u32[]{:S(2)}) collective-permute-start(bf16[64,1792]{1,0:T(8,128)(2,1)S(1)} %multiply_convert_fusion.2.refs_0_), channel_id=1, source_target_pairs={{0,64},{32,96},{64,0},{96,32},{1,65},{33,97},{65,1},{97,33},{2,66}... | collective-permute-start | bytes 688136 | tf_op jit(solution)/shard_map/ppermute | solution.py:19
  82.7 9.3 %collective-permute-start.14 = (bf16[64,1792]{1,0:T(8,128)(2,1)S(1)}, bf16[64,1792]{1,0:T(8,128)(2,1)S(1)}, u32[]{:S(2)}, u32[]{:S(2)}) collective-permute-start(bf16[64,1792]{1,0:T(8,128)(2,1)S(1)} %multiply_convert_fusion.2.refs_0_), channel_id=1, source_target_pairs={{0,96},{32,0},{64,32},{96,64},{1,97},{33,1},{65,33},{97,65},{2,98}... | collective-permute-start | bytes 688136 | tf_op jit(solution)/shard_map/ppermute | solution.py:19
  106.7 25.1 %all-to-all-start = ((bf16[8,256,256]{2,1,0:T(8,128)(2,1)}), bf16[8,256,256]{2,1,0:T(8,128)(2,1)}, u32[]{:S(2)}, u32[]{:S(2)}) async-start(bf16[8,256,256]{2,1,0:T(8,128)(2,1)} %copy-done.12), calls=%async_computation | async-start | bytes 2097152 | tf_op jit(solution)/shard_map/all_to_all | solution.py:331
  119.9 14.6 %collective-permute-start.24 = (bf16[3,256,896]{2,1,0:T(8,128)(2,1)S(1)}, bf16[3,256,896]{2,1,0:T(8,128)(2,1)}, u32[]{:S(2)}, u32[]{:S(2)}) collective-permute-start(bf16[3,256,896]{2,1,0:T(8,128)(2,1)S(1)} %collective-permute-done.10.refs_1_.refs_8_.refs_4_), channel_id=1, source_target_pairs={{0,8},{8,0},{16,24},{24,16},{1,9},{9,1},{17,25},{25,17},{2,10},{10... | collective-permute-start | bytes 4128776 | tf_op jit(solution)/shard_map/ppermute | solution.py:389
  119.9 17.1 %collective-permute-start.27 = (bf16[3,256,896]{2,1,0:T(8,128)(2,1)S(1)}, bf16[3,256,896]{2,1,0:T(8,128)(2,1)}, u32[]{:S(2)}, u32[]{:S(2)}) collective-permute-start(bf16[3,256,896]{2,1,0:T(8,128)(2,1)S(1)} %collective-permute-done.11.refs_4_.refs_11_.refs_7_), channel_id=1, source_target_pairs={{0,8},{8,0},{16,24},{24,16},{1,9},{9,1},{17,25},{25,17},{2,10},{10... | collective-permute-start | bytes 4128776 | tf_op jit(solution)/shard_map/ppermute | solution.py:389
  133.3 14.2 %collective-permute-start.25 = (bf16[3,256,896]{2,1,0:T(8,128)(2,1)}, bf16[3,256,896]{2,1,0:T(8,128)(2,1)S(1)}, u32[]{:S(2)}, u32[]{:S(2)}) collective-permute-start(bf16[3,256,896]{2,1,0:T(8,128)(2,1)} %collective-permute-done.15.refs_2_.refs_9_.refs_5_), channel_id=1, source_target_pairs={{0,8},{8,0},{16,24},{24,16},{1,9},{9,1},{17,25},{25,17},{2,10},{10... | collective-permute-start | bytes 4128776 | tf_op jit(solution)/shard_map/ppermute | solution.py:389
  133.4 16.3 %collective-permute-start.26 = (bf16[3,256,896]{2,1,0:T(8,128)(2,1)}, bf16[3,256,896]{2,1,0:T(8,128)(2,1)S(1)}, u32[]{:S(2)}, u32[]{:S(2)}) collective-permute-start(bf16[3,256,896]{2,1,0:T(8,128)(2,1)} %collective-permute-done.16.refs_3_.refs_10_.refs_6_), channel_id=1, source_target_pairs={{0,8},{8,0},{16,24},{24,16},{1,9},{9,1},{17,25},{25,17},{2,10},{10... | collective-permute-start | bytes 4128776 | tf_op jit(solution)/shard_map/ppermute | solution.py:389
  133.9 10.0 %collective-permute-start.17 = (bf16[256,256]{1,0:T(8,128)(2,1)S(1)}, bf16[256,256]{1,0:T(8,128)(2,1)S(1)}, u32[]{:S(2)}, u32[]{:S(2)}) collective-permute-start(bf16[256,256]{1,0:T(8,128)(2,1)S(1)} %add_convert_fusion.3.refs_0_), channel_id=1, source_target_pairs={{0,1},{1,2},{2,3},{3,4},{4,5},{5,6},{6,7},{7,0},{8,9},{9,10},{10,1... | collective-permute-start | bytes 393224 | tf_op jit(solution)/shard_map/ppermute | solution.py:19
  134.5 10.2 %collective-permute-start.18 = (bf16[256,256]{1,0:T(8,128)(2,1)S(1)}, bf16[256,256]{1,0:T(8,128)(2,1)S(1)}, u32[]{:S(2)}, u32[]{:S(2)}) collective-permute-start(bf16[256,256]{1,0:T(8,128)(2,1)S(1)} %add_convert_fusion.3.refs_0_), channel_id=1, source_target_pairs={{0,2},{1,3},{2,4},{3,5},{4,6},{5,7},{6,0},{7,1},{8,10},{9,11},{10,... | collective-permute-start | bytes 393224 | tf_op jit(solution)/shard_map/ppermute | solution.py:19
  137.0 19.2 %collective-permute-start.19 = (bf16[256,256]{1,0:T(8,128)(2,1)S(1)}, bf16[256,256]{1,0:T(8,128)(2,1)S(1)}, u32[]{:S(2)}, u32[]{:S(2)}) collective-permute-start(bf16[256,256]{1,0:T(8,128)(2,1)S(1)} %add_convert_fusion.3.refs_0_), channel_id=1, source_target_pairs={{0,3},{1,4},{2,5},{3,6},{4,7},{5,0},{6,1},{7,2},{8,11},{9,12},{10,... | collective-permute-start | bytes 393224 | tf_op jit(solution)/shard_map/ppermute | solution.py:19
  143.9 12.3 %collective-permute-start.20 = (bf16[256,256]{1,0:T(8,128)(2,1)S(1)}, bf16[256,256]{1,0:T(8,128)(2,1)S(1)}, u32[]{:S(2)}, u32[]{:S(2)}) collective-permute-start(bf16[256,256]{1,0:T(8,128)(2,1)S(1)} %add_convert_fusion.3.refs_0_), channel_id=1, source_target_pairs={{0,4},{1,5},{2,6},{3,7},{4,0},{5,1},{6,2},{7,3},{8,12},{9,13},{10,... | collective-permute-start | bytes 393224 | tf_op jit(solution)/shard_map/ppermute | solution.py:19
  144.8 11.5 %collective-permute-start.21 = (bf16[256,256]{1,0:T(8,128)(2,1)S(1)}, bf16[256,256]{1,0:T(8,128)(2,1)S(1)}, u32[]{:S(2)}, u32[]{:S(2)}) collective-permute-start(bf16[256,256]{1,0:T(8,128)(2,1)S(1)} %add_convert_fusion.3.refs_0_), channel_id=1, source_target_pairs={{0,5},{1,6},{2,7},{3,0},{4,1},{5,2},{6,3},{7,4},{8,13},{9,14},{10,... | collective-permute-start | bytes 393224 | tf_op jit(solution)/shard_map/ppermute | solution.py:19
  163.2 16.7 %collective-permute-start.33 = (bf16[2,64,896]{2,1,0:T(8,128)(2,1)}, bf16[2,64,896]{2,1,0:T(8,128)(2,1)}, u32[]{:S(2)}, u32[]{:S(2)}) collective-permute-start(bf16[2,64,896]{2,1,0:T(8,128)(2,1)} %get-tuple-element.133), channel_id=1, source_target_pairs={{0,96},{32,0},{64,32},{96,64},{1,97},{33,1},{65,33},{97,65},{2,98}... | collective-permute-start | bytes 688136 | tf_op jit(solution)/shard_map/ppermute | solution.py:19
  168.2 11.7 %collective-permute-start.32 = (bf16[2,64,896]{2,1,0:T(8,128)(2,1)}, bf16[2,64,896]{2,1,0:T(8,128)(2,1)}, u32[]{:S(2)}, u32[]{:S(2)}) collective-permute-start(bf16[2,64,896]{2,1,0:T(8,128)(2,1)} %get-tuple-element.132), channel_id=1, source_target_pairs={{0,64},{32,96},{64,0},{96,32},{1,65},{33,97},{65,1},{97,33},{2,66}... | collective-permute-start | bytes 688136 | tf_op jit(solution)/shard_map/ppermute | solution.py:19
  168.2 13.8 %collective-permute-start.31 = (bf16[2,64,896]{2,1,0:T(8,128)(2,1)}, bf16[2,64,896]{2,1,0:T(8,128)(2,1)}, u32[]{:S(2)}, u32[]{:S(2)}) collective-permute-start(bf16[2,64,896]{2,1,0:T(8,128)(2,1)} %get-tuple-element.131), channel_id=1, source_target_pairs={{0,32},{32,64},{64,96},{96,0},{1,33},{33,65},{65,97},{97,1},{2,34}... | collective-permute-start | bytes 688136 | tf_op jit(solution)/shard_map/ppermute | solution.py:19
  169.7 13.6 %collective-permute-start.30 = (bf16[64,896]{1,0:T(8,128)(2,1)}, bf16[64,896]{1,0:T(8,128)(2,1)S(1)}, u32[]{:S(2)}, u32[]{:S(2)}) collective-permute-start(bf16[64,896]{1,0:T(8,128)(2,1)} %copy-done.33), channel_id=1, source_target_pairs={{0,96},{32,0},{64,32},{96,64},{1,97},{33,1},{65,33},{97,65},{2,98}... | collective-permute-start | bytes 344072 | tf_op jit(solution)/shard_map/ppermute | solution.py:19
  172.2 11.4 %collective-permute-start.29 = (bf16[64,896]{1,0:T(8,128)(2,1)}, bf16[64,896]{1,0:T(8,128)(2,1)S(1)}, u32[]{:S(2)}, u32[]{:S(2)}) collective-permute-start(bf16[64,896]{1,0:T(8,128)(2,1)} %copy-done.32), channel_id=1, source_target_pairs={{0,64},{32,96},{64,0},{96,32},{1,65},{33,97},{65,1},{97,33},{2,66}... | collective-permute-start | bytes 344072 | tf_op jit(solution)/shard_map/ppermute | solution.py:19
  187.3 10.5 %collective-permute-start.34 = (bf16[3,64,896]{2,1,0:T(8,128)(2,1)S(1)}, bf16[3,64,896]{2,1,0:T(8,128)(2,1)S(1)}, u32[]{:S(2)}, u32[]{:S(2)}) collective-permute-start(bf16[3,64,896]{2,1,0:T(8,128)(2,1)S(1)} %pad_maximum_fusion.1.refs_0_), channel_id=1, source_target_pairs={{0,32},{32,64},{64,96},{96,0},{1,33},{33,65},{65,97},{97,1},{2,34}... | collective-permute-start | bytes 1032200 | tf_op jit(solution)/shard_map/ppermute | solution.py:19
  187.3 14.1 %collective-permute-start.35 = (bf16[3,64,896]{2,1,0:T(8,128)(2,1)S(1)}, bf16[3,64,896]{2,1,0:T(8,128)(2,1)S(1)}, u32[]{:S(2)}, u32[]{:S(2)}) collective-permute-start(bf16[3,64,896]{2,1,0:T(8,128)(2,1)S(1)} %pad_maximum_fusion.1.refs_0_), channel_id=1, source_target_pairs={{0,64},{32,96},{64,0},{96,32},{1,65},{33,97},{65,1},{97,33},{2,66}... | collective-permute-start | bytes 1032200 | tf_op jit(solution)/shard_map/ppermute | solution.py:19
  191.6 9.9 %collective-permute-start.36 = (bf16[3,64,896]{2,1,0:T(8,128)(2,1)S(1)}, bf16[3,64,896]{2,1,0:T(8,128)(2,1)S(1)}, u32[]{:S(2)}, u32[]{:S(2)}) collective-permute-start(bf16[3,64,896]{2,1,0:T(8,128)(2,1)S(1)} %pad_maximum_fusion.1.refs_0_), channel_id=1, source_target_pairs={{0,96},{32,0},{64,32},{96,64},{1,97},{33,1},{65,33},{97,65},{2,98}... | collective-permute-start | bytes 1032200 | tf_op jit(solution)/shard_map/ppermute | solution.py:19
  209.1 18.3 %all-to-all-start.1 = ((bf16[8,256,256]{2,1,0:T(8,128)(2,1)}), bf16[8,256,256]{2,1,0:T(8,128)(2,1)}, u32[]{:S(2)}, u32[]{:S(2)}) async-start(bf16[8,256,256]{2,1,0:T(8,128)(2,1)} %copy-done.13), calls=%async_computation.1 | async-start | bytes 2097152 | tf_op jit(solution)/shard_map/all_to_all | solution.py:331
  215.8 104.5 %reduce-scatter.2.cloned.1.call-start = ((), (), s32[]{:S(2)}) async-start(), calls=%async_computation.4 | async-start | bytes 2359296 | tf_op jit(solution)/shard_map/reduce_scatter | solution.py:462
  233.2 12.3 %collective-permute-start.39 = (bf16[256,256]{1,0:T(8,128)(2,1)S(1)}, bf16[256,256]{1,0:T(8,128)(2,1)S(1)}, u32[]{:S(2)}, u32[]{:S(2)}) collective-permute-start(bf16[256,256]{1,0:T(8,128)(2,1)S(1)} %add_convert_fusion.2.refs_0_), channel_id=1, source_target_pairs={{0,3},{1,4},{2,5},{3,6},{4,7},{5,0},{6,1},{7,2},{8,11},{9,12},{10,... | collective-permute-start | bytes 393224 | tf_op jit(solution)/shard_map/ppermute | solution.py:19
  235.1 10.4 %collective-permute-start.40 = (bf16[256,256]{1,0:T(8,128)(2,1)S(1)}, bf16[256,256]{1,0:T(8,128)(2,1)S(1)}, u32[]{:S(2)}, u32[]{:S(2)}) collective-permute-start(bf16[256,256]{1,0:T(8,128)(2,1)S(1)} %add_convert_fusion.2.refs_0_), channel_id=1, source_target_pairs={{0,4},{1,5},{2,6},{3,7},{4,0},{5,1},{6,2},{7,3},{8,12},{9,13},{10,... | collective-permute-start | bytes 393224 | tf_op jit(solution)/shard_map/ppermute | solution.py:19
  235.8 11.6 %collective-permute-start.41 = (bf16[256,256]{1,0:T(8,128)(2,1)S(1)}, bf16[256,256]{1,0:T(8,128)(2,1)S(1)}, u32[]{:S(2)}, u32[]{:S(2)}) collective-permute-start(bf16[256,256]{1,0:T(8,128)(2,1)S(1)} %add_convert_fusion.2.refs_0_), channel_id=1, source_target_pairs={{0,5},{1,6},{2,7},{3,0},{4,1},{5,2},{6,3},{7,4},{8,13},{9,14},{10,... | collective-permute-start | bytes 393224 | tf_op jit(solution)/shard_map/ppermute | solution.py:19
  238.6 13.2 %collective-permute-start.42 = (bf16[256,256]{1,0:T(8,128)(2,1)S(1)}, bf16[256,256]{1,0:T(8,128)(2,1)S(1)}, u32[]{:S(2)}, u32[]{:S(2)}) collective-permute-start(bf16[256,256]{1,0:T(8,128)(2,1)S(1)} %add_convert_fusion.2.refs_0_), channel_id=1, source_target_pairs={{0,6},{1,7},{2,0},{3,1},{4,2},{5,3},{6,4},{7,5},{8,14},{9,15},{10,... | collective-permute-start | bytes 393224 | tf_op jit(solution)/shard_map/ppermute | solution.py:19
  239.5 16.0 %collective-permute-start.43 = (bf16[256,256]{1,0:T(8,128)(2,1)S(1)}, bf16[256,256]{1,0:T(8,128)(2,1)S(1)}, u32[]{:S(2)}, u32[]{:S(2)}) collective-permute-start(bf16[256,256]{1,0:T(8,128)(2,1)S(1)} %add_convert_fusion.2.refs_0_), channel_id=1, source_target_pairs={{0,7},{1,0},{2,1},{3,2},{4,3},{5,4},{6,5},{7,6},{8,15},{9,8},{10,9... | collective-permute-start | bytes 393224 | tf_op jit(solution)/shard_map/ppermute | solution.py:19
  258.4 9.1 %collective-permute-start.44 = (bf16[64,1792]{1,0:T(8,128)(2,1)S(1)}, bf16[64,1792]{1,0:T(8,128)(2,1)S(1)}, u32[]{:S(2)}, u32[]{:S(2)}) collective-permute-start(bf16[64,1792]{1,0:T(8,128)(2,1)S(1)} %get-tuple-element.150), channel_id=1, source_target_pairs={{0,32},{32,64},{64,96},{96,0},{1,33},{33,65},{65,97},{97,1},{2,34}... | collective-permute-start | bytes 688136 | tf_op jit(solution)/shard_map/ppermute | solution.py:19
  259.0 13.8 %collective-permute-start.45 = (bf16[64,1792]{1,0:T(8,128)(2,1)S(1)}, bf16[64,1792]{1,0:T(8,128)(2,1)S(1)}, u32[]{:S(2)}, u32[]{:S(2)}) collective-permute-start(bf16[64,1792]{1,0:T(8,128)(2,1)S(1)} %get-tuple-element.151), channel_id=1, source_target_pairs={{0,64},{32,96},{64,0},{96,32},{1,65},{33,97},{65,1},{97,33},{2,66}... | collective-permute-start | bytes 688136 | tf_op jit(solution)/shard_map/ppermute | solution.py:19
  263.9 11.4 %collective-permute-start.46 = (bf16[64,1792]{1,0:T(8,128)(2,1)S(1)}, bf16[64,1792]{1,0:T(8,128)(2,1)S(1)}, u32[]{:S(2)}, u32[]{:S(2)}) collective-permute-start(bf16[64,1792]{1,0:T(8,128)(2,1)S(1)} %get-tuple-element.152), channel_id=1, source_target_pairs={{0,96},{32,0},{64,32},{96,64},{1,97},{33,1},{65,33},{97,65},{2,98}... | collective-permute-start | bytes 688136 | tf_op jit(solution)/shard_map/ppermute | solution.py:19
  275.8 10.2 %collective-permute-start.47 = (bf16[2,64,1792]{2,1,0:T(8,128)(2,1)S(1)}, bf16[2,64,1792]{2,1,0:T(8,128)(2,1)S(1)}, u32[]{:S(2)}, u32[]{:S(2)}) collective-permute-start(bf16[2,64,1792]{2,1,0:T(8,128)(2,1)S(1)} %pad_maximum_fusion.refs_0_), channel_id=1, source_target_pairs={{0,32},{32,64},{64,96},{96,0},{1,33},{33,65},{65,97},{97,1},{2,34}... | collective-permute-start | bytes 1376264 | tf_op jit(solution)/shard_map/ppermute | solution.py:19
  275.8 16.5 %collective-permute-start.48 = (bf16[2,64,1792]{2,1,0:T(8,128)(2,1)S(1)}, bf16[2,64,1792]{2,1,0:T(8,128)(2,1)S(1)}, u32[]{:S(2)}, u32[]{:S(2)}) collective-permute-start(bf16[2,64,1792]{2,1,0:T(8,128)(2,1)S(1)} %pad_maximum_fusion.refs_0_), channel_id=1, source_target_pairs={{0,64},{32,96},{64,0},{96,32},{1,65},{33,97},{65,1},{97,33},{2,66}... | collective-permute-start | bytes 1376264 | tf_op jit(solution)/shard_map/ppermute | solution.py:19
  281.0 11.4 %collective-permute-start.49 = (bf16[2,64,1792]{2,1,0:T(8,128)(2,1)S(1)}, bf16[2,64,1792]{2,1,0:T(8,128)(2,1)S(1)}, u32[]{:S(2)}, u32[]{:S(2)}) collective-permute-start(bf16[2,64,1792]{2,1,0:T(8,128)(2,1)S(1)} %pad_maximum_fusion.refs_0_), channel_id=1, source_target_pairs={{0,96},{32,0},{64,32},{96,64},{1,97},{33,1},{65,33},{97,65},{2,98}... | collective-permute-start | bytes 1376264 | tf_op jit(solution)/shard_map/ppermute | solution.py:19
  (44 other events, 290.7 us)
Sparse Core Ops, SparseCore 0:
  54.7 64.8 all-gather.2
  229.8 44.1 reduce-scatter.1
